TPU v7x, 512 devices: a whole 4x8x8 slice. The times are simulated.
512 devices in a mesh: row: 32 (over x, z), col: 16 (over y, core).
Axes of the slice: x: 4, y: 8, z: 8, core: 2. Of those that a mesh axis runs over, the one named last changes fastest.
Arguments:
- load: float32 [3, 557568], P(None, ('row', 'col')), may hold values from -6 to 6
- node_mass: float32 [557568], P(('row', 'col')), may hold values from 0.05 to 0.5
- side_lists: int32 [2, 16896], P(None, ('row', 'col')), may hold values from 0 to 1088, as said below
- end_lists: int32 [2, 16896], P(None, ('row', 'col')), may hold values from 0 to 1088, as said below
- connect: int32 [3, 1048576], P(None, ('row', 'col')), may hold values from 0 to 1088, as said below
- geometry: float32 [4, 1048576], P(None, ('row', 'col')), may hold values from -4 to 4
- cover: float32 [1048576], P(('row', 'col')), may hold values from 0.1 to 2
- grazing: float32 [1048576], P(('row', 'col')), may hold values from 0 to 1
- rates: float32 [3], replicated, may hold values from 0.5 to 3
- elem_count: int32 [512], P(('row', 'col')), may hold values from 682 to 2048, as said below
- basis: float32 [32, 557568], P(None, ('row', 'col')), may hold values from -0.1875 to 0.1875
- coarse_inverse: bfloat16 [16384, 16384], P(('row', 'col')), as said below
Outputs:
- solution: float32 [3, 557568], P(None, ('row', 'col'))
- residual: float32 [3, 557568], P(None, ('row', 'col'))
- precond: float32 [3, 557568], P(None, ('row', 'col'))
Inputs may be any that keep to these rules, and one draw needn't show every extreme that they name: connect holds local node numbers; each subdomain is a triangulated grid of 33 x 33 nodes with its nodes and elements numbered in a scattered order. side_lists[0] and side_lists[1] of a subdomain list its two edges toward the previous and next subdomain along col, each in an order that matches the neighbour's opposite list entry by entry; end_lists likewise along row; a corner node stands in one side list and one end list. `side_lists`: see connect. `end_lists`: see connect. A subdomain's live elements are its first elem_count slots; at least one subdomain is full and one holds the fewest. `coarse_inverse`: symmetric positive definite.
All inputs are finite; a program needn't handle non-finite values.
Results may differ from a plain program's by a relative error of at most 0.0003.
Values sent between devices are 32-bit elements; how exact they have to be, the bound alone decides.
A program may use at most 64 MiB of HBM per device.

v0:
```python
import jax
import jax.numpy as jnp
from jax import lax
from jax.sharding import PartitionSpec as P

ITERS = 2


highest = lax.Precision.HIGHEST


def with_halo(cells, sides, width):
    for axis, dim in sides:
        count = lax.axis_size(axis)
        ends = count - 1
        head = lax.slice_in_dim(cells, 0, width, axis=dim)
        tail = lax.slice_in_dim(cells, cells.shape[dim] - width, cells.shape[dim], axis=dim)
        cells = jnp.concatenate(
            [
                lax.ppermute(tail, axis, [(i, (i + 1) % count) for i in range(ends)]),
                cells,
                lax.ppermute(head, axis, [((i + 1) % count, i) for i in range(ends)]),
            ],
            axis=dim,
        )
    return cells


def assemble(vectors, side_lists, end_lists):
    packed = jnp.stack([vectors[:, side_lists[0]], vectors[:, side_lists[1]]])
    padded = with_halo(packed, (("col", 0),), 1)
    vectors = vectors.at[:, side_lists[0]].add(padded[0]).at[:, side_lists[1]].add(padded[3])
    packed = jnp.stack([vectors[:, end_lists[0]], vectors[:, end_lists[1]]])
    padded = with_halo(packed, (("row", 0),), 1)
    return vectors.at[:, end_lists[0]].add(padded[0]).at[:, end_lists[1]].add(padded[3])


def gradients(geometry):
    b_terms = jnp.stack([geometry[0], geometry[1], -geometry[0] - geometry[1]])
    c_terms = jnp.stack([geometry[2], geometry[3], -geometry[2] - geometry[3]])
    return (b_terms, c_terms)


def element_terms(vector, connect, b_terms, c_terms, conduct, summed):
    corner = vector[:, connect]
    along_x = jnp.sum(b_terms[None] * corner, axis=1)
    along_y = jnp.sum(c_terms[None] * corner, axis=1)
    element_term = conduct[:, None, :] * (
        b_terms[None] * along_x[:, None, :] + c_terms[None] * along_y[:, None, :]
    )
    return summed.at[:, connect.reshape(-1)].add(element_term.reshape(vector.shape[0], -1))


def body(
    load,
    node_mass,
    side_lists,
    end_lists,
    connect,
    geometry,
    cover,
    grazing,
    rates,
    elem_count,
    basis,
    coarse_inverse,
):
    samples = load.shape[0]
    elements = connect.shape[1]
    inverse_wide = coarse_inverse.astype(jnp.float32)
    b_terms, c_terms = gradients(geometry)
    live_mask = (lax.iota(jnp.int32, elements) < elem_count[0]).astype(jnp.float32)
    conduct = cover[None, :] * jnp.exp(-rates[:, None] * grazing[None, :]) * live_mask[None, :]
    diag_terms = conduct[:, None, :] * (b_terms * b_terms + c_terms * c_terms)[None]
    diag_sum = jnp.zeros_like(load).at[:, connect.reshape(-1)].add(diag_terms.reshape(samples, -1))
    diag_local = node_mass[None, :] + diag_sum
    stacked = assemble(
        jnp.concatenate([load, diag_local, jnp.ones_like(node_mass)[None]], axis=0),
        side_lists,
        end_lists,
    )
    right_side = stacked[:samples]
    diagonal = stacked[samples : 2 * samples]
    weight = 1.0 / stacked[2 * samples]

    def precondition(residual):
        coarse_rhs = jnp.dot(weight[None, :] * residual, basis.T, precision=highest)
        coarse_sol = jnp.dot(
            lax.all_gather(coarse_rhs, ("row", "col"), axis=1, tiled=True),
            inverse_wide.T,
            precision=highest,
        )
        spread = jnp.dot(coarse_sol, basis, precision=highest) * weight[None, :]
        return residual / diagonal + assemble(spread, side_lists, end_lists)

    def fit_sum(first, second):
        return lax.psum(jnp.sum(weight[None, :] * first * second, axis=1), ("row", "col"))

    solution = jnp.zeros_like(right_side)
    residual = right_side
    precond = precondition(residual)
    fit_now = fit_sum(residual, precond)
    direction = precond
    for sweep in range(ITERS):
        start_sum = node_mass[None, :] * direction
        local_sum = element_terms(direction, connect, b_terms, c_terms, conduct, start_sum)
        image = assemble(local_sum, side_lists, end_lists)
        curved = lax.psum(jnp.sum(weight[None, :] * direction * image, axis=1), ("row", "col"))
        step_size = fit_now / curved
        solution = solution + step_size[:, None] * direction
        residual = residual - step_size[:, None] * image
        precond = precondition(residual)
        if sweep + 1 < ITERS:
            fit_next = fit_sum(residual, precond)
            direction = precond + (fit_next / fit_now)[:, None] * direction
            fit_now = fit_next
    return (solution, residual, precond)


def solution(mesh):
    return jax.shard_map(
        body,
        mesh=mesh,
        in_specs=(
            P(None, ("row", "col")),
            P(("row", "col")),
            P(None, ("row", "col")),
            P(None, ("row", "col")),
            P(None, ("row", "col")),
            P(None, ("row", "col")),
            P(("row", "col")),
            P(("row", "col")),
            P(),
            P(("row", "col")),
            P(None, ("row", "col")),
            P(("row", "col"), None),
        ),
        out_specs=(P(None, ("row", "col")), P(None, ("row", "col")), P(None, ("row", "col"))),
        check_vma=False,
    )
```

profile of v0, /device:TPU:1, one launch (start us, length us, event | category | flops | bytes accessed | tf_op | source)
XLA Modules:
  0.0 868.7 jit_solution(13365342400787217694)
XLA Ops:
  7.6 2.5 bitcast_multiply_fusion.2
  10.4 33.9 %scatter_custom_fusion = f32[3,1089]{0,1:T(8,128)S(1)} fusion(f32[3,1089]{0,1:T(8,128)S(1)} %add.208.clone, s32[6144]{0:T(1024)S(1)} %bitcast.263, f32[3,6144]{0,1:T(8,128)} %bitcast_multiply_fusion.2), kind=kCustom, calls=%fused_computation.66 | custom fusion | flops 18432 | bytes 86796 | tf_op jit(solution)/shard_map/scatter-add | solution.py:75
  45.1 1.4 pad_maximum_fusion
  47.2 4.6 collective-permute-start
  52.3 5.5 collective-permute-start.1
  60.5 2.5 collective-permute-start.2
  63.5 1.3 collective-permute-start.3
  65.8 2.9 collective-permute-done.3
  71.4 81.3 %all-gather = f32[512,32,3]{1,2,0:T(4,128)S(1)} all-gather(f32[1,32,3]{1,2,0:T(4,128)S(1)} %convolution_bitcast_fusion.2), channel_id=1, replica_groups=mesh['row'=32,'col'=16] {'row','col'}, dimensions={0}, use_global_device_ids=true | all-gather | bytes 196992 | tf_op jit(solution)/shard_map/all_gather | solution.py:89
  156.1 3.7 collective-permute-start.4
  159.9 1.9 collective-permute-start.5
  161.8 1.3 copy.403
  167.5 1.6 collective-permute-start.6
  169.1 1.3 collective-permute-start.7
  170.8 2.7 collective-permute-done.7
  175.8 20.9 %gather_fusion.8 = f32[6144,3]{1,0:T(8,128)} fusion(f32[3,1089]{0,1:T(8,128)S(1)} %scatter_fusion.3, s32[6144]{0:T(1024)S(1)} %broadcast_clamp_fusion), kind=kCustom, calls=%fused_computation.8 | custom fusion | bytes 172032 | tf_op jit(solution)/shard_map/gather | solution.py:45
  196.7 4.9 multiply_reduce_fusion.3
  202.6 4.6 bitcast_multiply_fusion.1
  207.2 35.5 %scatter_custom_fusion.9 = f32[3,1089]{0,1:T(8,128)} fusion(f32[3,1089]{0,1:T(8,128)} %copy.346, s32[6144]{0:T(1024)} %bitcast.264, f32[3,6144]{0,1:T(8,128)} %bitcast_multiply_fusion.1), kind=kCustom, calls=%fused_computation.61 | custom fusion | flops 18432 | bytes 3158796 | tf_op jit(solution)/shard_map/scatter-add | solution.py:51
  242.7 1.7 gather_fusion.9
  244.5 1.7 gather_fusion.10
  246.3 4.4 collective-permute-start.8
  250.8 1.9 collective-permute-start.9
  252.8 2.6 scatter_fusion.4
  255.8 2.6 scatter_fusion.5
  258.4 1.7 gather_fusion.11
  260.1 1.7 gather_fusion.12
  261.9 2.8 collective-permute-start.10
  264.9 1.3 collective-permute-start.11
  266.3 2.6 scatter_fusion.6
  269.6 2.6 scatter_fusion.7
  273.5 102.2 %all-reduce = (f32[3]{0:T(128)S(1)}, f32[3]{0:T(128)S(1)}) all-reduce(f32[3]{0:T(128)S(1)} %get-tuple-element.23, f32[3]{0:T(128)S(1)} %get-tuple-element.22), channel_id=1, replica_groups=mesh['row'=32,'col'=16] {'row','col'}, use_global_device_ids=true, to_apply=%region_10.0 | all-reduce | flops 6 | bytes 48 | tf_op jit(solution)/shard_map/psum | solution.py:97
  377.1 73.0 %all-gather.1 = f32[512,32,3]{1,2,0:T(4,128)S(1)} all-gather(f32[1,32,3]{1,2,0:T(4,128)S(1)} %convolution_bitcast_fusion.1), channel_id=1, replica_groups=mesh['row'=32,'col'=16] {'row','col'}, dimensions={0}, use_global_device_ids=true | all-gather | bytes 196992 | tf_op jit(solution)/shard_map/all_gather | solution.py:89
  453.4 3.7 collective-permute-start.12
  457.2 1.9 collective-permute-start.13
  460.2 2.0 collective-permute-done.13
  464.8 1.3 collective-permute-start.14
  466.3 1.3 collective-permute-start.15
  467.9 2.7 collective-permute-done.15
  472.9 101.1 %psum.30 = f32[3]{0:T(128)S(1)} all-reduce(f32[3]{0:T(128)S(1)} %multiply_reduce_fusion.5), channel_id=1, replica_groups=mesh['row'=32,'col'=16] {'row','col'}, use_global_device_ids=true, to_apply=%region_25.0 | all-reduce | flops 3 | bytes 24 | tf_op jit(solution)/shard_map/psum | solution.py:97
  574.9 20.9 %gather_fusion.17 = f32[6144,3]{1,0:T(8,128)} fusion(f32[3,1089]{0,1:T(8,128)S(1)} %copy.375, s32[6144]{0:T(1024)S(1)} %broadcast_clamp_fusion), kind=kCustom, calls=%fused_computation.17 | custom fusion | bytes 172032 | tf_op jit(solution)/shard_map/gather | solution.py:45
  595.8 4.9 multiply_reduce_fusion.1
  601.7 4.6 bitcast_multiply_fusion
  606.3 35.5 %scatter_custom_fusion.18 = f32[3,1089]{0,1:T(8,128)} fusion(f32[3,1089]{0,1:T(8,128)} %copy.376, s32[6144]{0:T(1024)} %bitcast.265, f32[3,6144]{0,1:T(8,128)} %bitcast_multiply_fusion), kind=kCustom, calls=%fused_computation.56 | custom fusion | flops 18432 | bytes 3158796 | tf_op jit(solution)/shard_map/scatter-add | solution.py:51
  641.9 1.7 gather_fusion.18
  643.6 1.7 gather_fusion.19
  645.4 2.3 collective-permute-start.16
  647.9 2.0 collective-permute-start.17
  650.0 2.6 scatter_fusion.12
  652.9 2.6 scatter_fusion.13
  655.4 1.7 gather_fusion.20
  657.2 1.7 gather_fusion.21
  659.0 3.5 collective-permute-start.18
  662.6 1.3 collective-permute-start.19
  664.0 2.6 scatter_fusion.14
  667.0 2.6 scatter_fusion.15
  671.0 100.6 %psum.31 = f32[3]{0:T(128)S(1)} all-reduce(f32[3]{0:T(128)S(1)} %multiply_reduce_fusion.4), channel_id=1, replica_groups=mesh['row'=32,'col'=16] {'row','col'}, use_global_device_ids=true, to_apply=%region_34.0 | all-reduce | flops 3 | bytes 24 | tf_op jit(solution)/shard_map/psum | solution.py:108
  772.5 73.0 %all-gather.2 = f32[512,32,3]{1,2,0:T(4,128)S(1)} all-gather(f32[1,32,3]{1,2,0:T(4,128)S(1)} %convolution_bitcast_fusion), channel_id=1, replica_groups=mesh['row'=32,'col'=16] {'row','col'}, dimensions={0}, use_global_device_ids=true | all-gather | bytes 196992 | tf_op jit(solution)/shard_map/all_gather | solution.py:89
  848.8 3.6 collective-permute-start.20
  852.5 1.9 collective-permute-start.21
  855.4 2.0 collective-permute-done.21
  860.1 1.4 collective-permute-start.22
  861.6 1.3 collective-permute-start.23
  863.3 2.6 collective-permute-done.23
  (217 shorter events, 57.0 us)
Async XLA Ops:
  0.6 152.6 %copy-start = (bf16[32,16384]{1,0:T(8,128)(2,1)S(1)}, bf16[32,16384]{1,0:T(8,128)(2,1)}, u32[]{:S(2)}) copy-start(bf16[32,16384]{1,0:T(8,128)(2,1)} %param.23) | copy-start | bytes 3145732
  1.5 8.7 copy-start.5
  3.2 456.0 %copy-start.11 = (s32[33]{0:T(128)}, s32[33]{0:T(128)S(1)}, u32[]{:S(2)}) copy-start(s32[33]{0:T(128)S(1)} %get-tuple-element.39) | copy-start | bytes 400
  3.3 459.0 %copy-start.7 = (s32[33]{0:T(128)}, s32[33]{0:T(128)S(1)}, u32[]{:S(2)}) copy-start(s32[33]{0:T(128)S(1)} %get-tuple-element.38) | copy-start | bytes 400
  6.6 37.7 %copy-start.16 = (s32[6144,1]{0,1:T(1,128)}, s32[6144,1]{0,1:T(1,128)S(1)}, u32[]{:S(2)}) copy-start(s32[6144,1]{0,1:T(1,128)S(1)} %compare_select_fusion) | copy-start | bytes 73732
  7.6 39.0 %copy-start.18 = (s32[1024]{0:T(1024)}, s32[1024]{0:T(1024)S(1)}, u32[]{:S(2)}) copy-start(s32[1024]{0:T(1024)S(1)} %get-tuple-element.45) | copy-start | bytes 12292
  7.6 44.1 %copy-start.17 = (s32[1024]{0:T(1024)}, s32[1024]{0:T(1024)S(1)}, u32[]{:S(2)}) copy-start(s32[1024]{0:T(1024)S(1)} %get-tuple-element.44) | copy-start | bytes 12292
  10.4 47.4 %copy-start.4 = (s32[3,2048]{1,0:T(4,128)S(1)}, s32[3,2048]{1,0:T(4,128)}, u32[]{:S(2)}) copy-start(s32[3,2048]{1,0:T(4,128)} %param.16) | copy-start | bytes 73732
  10.4 47.5 %copy-start.23 = (s32[2,33]{1,0:T(2,128)S(1)}, s32[2,33]{1,0:T(2,128)}, u32[]{:S(2)}) copy-start(s32[2,33]{1,0:T(2,128)} %param.15) | copy-start | bytes 796
  44.3 0.8 copy-start.2
  46.6 24.7 %copy-start.1 = (f32[32,1089]{1,0:T(8,128)S(1)}, f32[32,1089]{1,0:T(8,128)}, u32[]{:S(2)}) copy-start(f32[32,1089]{1,0:T(8,128)} %param.22) | copy-start | bytes 418180
  47.2 10.9 %collective-permute-start = (f32[1,7,33]{1,2,0:T(8,128)S(1)}, f32[1,7,33]{1,2,0:T(8,128)S(1)}, u32[]{:S(2)}, u32[]{:S(2)}) collective-permute-start(f32[1,7,33]{1,2,0:T(8,128)S(1)} %bitcast.307), channel_id=1, source_target_pairs={{0,1},{1,2},{2,3},{3,4},{4,5},{5,6},{6,7},{7,8},{8,9},{9,10},{10,1... | collective-permute-start | bytes 2780 | tf_op jit(solution)/shard_map/ppermute | solution.py:20
  52.3 6.6 collective-permute-start.1
  57.9 94.9 %copy-start.13 = (s32[33]{0:T(128)}, s32[33]{0:T(128)S(1)}, u32[]{:S(2)}) copy-start(s32[33]{0:T(128)S(1)} %get-tuple-element.37) | copy-start | bytes 400
  57.9 413.7 %copy-start.9 = (s32[33]{0:T(128)}, s32[33]{0:T(128)S(1)}, u32[]{:S(2)}) copy-start(s32[33]{0:T(128)S(1)} %get-tuple-element.36) | copy-start | bytes 400
  58.0 2.5 copy-start.20
  58.0 5.5 copy-start.19
  60.5 4.4 collective-permute-start.2
  63.5 5.2 collective-permute-start.3
  152.8 20.7 %copy-start.14 = (s32[33]{0:T(128)S(1)}, s32[33]{0:T(128)}, u32[]{:S(2)}) copy-start(s32[33]{0:T(128)} %copy-done.13) | copy-start | bytes 400
  156.1 7.0 collective-permute-start.4
  159.9 4.9 collective-permute-start.5
  167.5 3.2 collective-permute-start.6
  169.1 4.3 collective-permute-start.7
  246.3 6.4 collective-permute-start.8
  250.8 4.9 collective-permute-start.9
  261.9 4.2 collective-permute-start.10
  264.9 4.6 collective-permute-start.11
  375.7 0.5 copy-start.26
  376.2 0.6 copy-start.21
  450.6 123.4 %copy-start.27 = (f32[3]{0:T(128)S(1)}, f32[3]{0:T(128)}, u32[]{:S(2)}) copy-start(f32[3]{0:T(128)} %copy-done.26) | copy-start | bytes 40
  453.4 5.7 collective-permute-start.12
  457.2 4.9 collective-permute-start.13
  464.8 3.0 collective-permute-start.14
  466.3 4.3 collective-permute-start.15
  574.0 26.7 %copy-start.24 = (f32[3]{0:T(128)}, f32[3]{0:T(128)S(1)}, u32[]{:S(2)}) copy-start(f32[3]{0:T(128)S(1)} %psum.30) | copy-start | bytes 40
  574.9 25.8 %copy-start.6 = (f32[3,1089]{1,0:T(4,128)S(1)}, f32[3,1089]{1,0:T(4,128)}, u32[]{:S(2)}) copy-start(f32[3,1089]{1,0:T(4,128)} %get-tuple-element.26) | copy-start | bytes 39208
  606.3 43.6 %copy-start.12 = (s32[33]{0:T(128)S(1)}, s32[33]{0:T(128)}, u32[]{:S(2)}) copy-start(s32[33]{0:T(128)} %copy-done.11) | copy-start | bytes 400
  606.3 46.5 %copy-start.8 = (s32[33]{0:T(128)S(1)}, s32[33]{0:T(128)}, u32[]{:S(2)}) copy-start(s32[33]{0:T(128)} %copy-done.7) | copy-start | bytes 400
  606.3 60.7 %copy-start.10 = (s32[33]{0:T(128)S(1)}, s32[33]{0:T(128)}, u32[]{:S(2)}) copy-start(s32[33]{0:T(128)} %copy-done.9) | copy-start | bytes 400
  606.3 165.3 %copy-start.25 = (f32[3]{0:T(128)S(1)}, f32[3]{0:T(128)}, u32[]{:S(2)}) copy-start(f32[3]{0:T(128)} %copy-done.24) | copy-start | bytes 40
  606.3 165.3 %copy-start.22 = (f32[3]{0:T(128)S(1)}, f32[3]{0:T(128)}, u32[]{:S(2)}) copy-start(f32[3]{0:T(128)} %copy-done.21) | copy-start | bytes 40
  645.4 4.4 collective-permute-start.16
  647.9 4.9 collective-permute-start.17
  659.0 4.9 collective-permute-start.18
  662.6 4.3 collective-permute-start.19
  772.3 90.6 %copy-start.3 = (f32[3,1089]{1,0:T(4,128)}, f32[3,1089]{1,0:T(4,128)S(1)}, u32[]{:S(2)}) copy-start(f32[3,1089]{1,0:T(4,128)S(1)} %get-tuple-element.40) | copy-start | bytes 39208
  845.5 20.6 %copy-start.15 = (s32[33]{0:T(128)S(1)}, s32[33]{0:T(128)}, u32[]{:S(2)}) copy-start(s32[33]{0:T(128)} %copy-done.13) | copy-start | bytes 400
  848.8 5.6 collective-permute-start.20
  852.5 4.9 collective-permute-start.21
  860.1 3.1 collective-permute-start.22
  861.6 4.3 collective-permute-start.23
where the time goes:
time: 874 us; the launch traced here: 869 us
  blocking collectives  531 us (61%)
  other arithmetic  169 us (19%)
  local copies, waits for them, and re-layouts  87.5 us (10%)
  starting transfers between devices  58.2 us (7%)
  waiting for transfers between devices  17 us (2%)
    all_gather x3, blocking collectives, precondition(): lax.all_gather(coarse_rhs, ('row', 'col'), axis=1, tiled=True)  227 us
    psum x2, blocking collectives, fit_sum(): lax.psum(jnp.sum(weight[None, :] * first * second, axis=1), ('row', 'col'))  203 us
    psum x1, blocking collectives, body(): lax.psum(jnp.sum(weight[None, :] * direction * image, axis=1), ('row', 'c...  101 us
    scatter-add x2, other arithmetic, element_terms(): summed.at[:, connect.reshape(-1)]  71 us
    gather x2, local copies, waits for them, and re-layouts, element_terms(): corner = vector[:, connect]  41.8 us
    ppermute x12, starting transfers between devices, with_halo(): lax.ppermute(tail, axis, [(i, (i + 1) % count) for i in range(ends)])  35.4 us
    scatter-add x1, other arithmetic, body(): jnp.zeros_like(load).at[:, connect.reshape(-1)]  33.9 us
    ppermute x12, starting transfers between devices, with_halo(): lax.ppermute(head, axis, [((i + 1) % count, i) for i in range(ends)])  22.8 us
  transfers between devices with their start and end apart: 24, of which 11 were waited for; matrix products, arithmetic and copies ran while one was open for 2% of the time, Pallas kernels for 0%

commit v1 on v0

v1 whole, which is shorter than its diff:
```python
import functools

import jax
import jax.numpy as jnp
from jax import lax
from jax.experimental import pallas as pl
from jax.experimental.pallas import tpu as pltpu
from jax.sharding import PartitionSpec as P

MESH = pl.DeviceIdType.MESH
F32, BF16, I32 = jnp.float32, jnp.bfloat16, jnp.int32

NX, NZ, NY = 4, 8, 8
N_ROW, N_COL = 32, 16
SIDE, NL, EL, NC, SAMPLES = 33, 1089, 2048, 32, 3
NH = 9
GAP = 40
EMPTY = 36
AROUND = ((-1, -1), (-1, 1), (1, -1), (1, 1), (-1, 0), (1, 0), (0, -1), (0, 1))
HALOS = 7


def take(row, index):
    return jnp.take_along_axis(
        jnp.broadcast_to(row, index.shape), index, axis=1, mode="promise_in_bounds"
    )


def halves(value):
    high = value.astype(BF16)
    return high, (value - high.astype(F32)).astype(BF16)


def dot_lanes(left, right):
    return lax.dot_general(left, right, (((1,), (1,)), ((), ())), preferred_element_type=F32)


def dot_rows(left, right):
    return lax.dot_general(left, right, (((1,), (0,)), ((), ())), preferred_element_type=F32)


def over_groups(row):
    row = row + pltpu.roll(row, 64, 1)
    return row + pltpu.roll(row, 32, 1)


def kernel(
    load_ref, mass_ref, side_ref, end_ref, side_sm, end_sm, conn_ref, geom_ref, cover_ref, graze_ref,
    rates_sm, count_sm, basis_hbm, inv_hbm,
    sol_ref, res_ref, pre_ref,
    basis_ref, inv_ref, low_ref, high_ref, geo_ref, cond_ref, piece_ref, left_ref, hot_ref,
    mass_vm, slot_ref, list_ref, wide_ref, spread_ref, coarse_ref, all_ref, first_ref, node_ref,
    halo_out, halo_in,
    local_sem, hs_sem, hr_sem, ys_sem, yr_sem, zs_sem, zr_sem, xs_sem, xr_sem, cs_sem, cr_sem,
):
    row, col = lax.axis_index("row"), lax.axis_index("col")
    x, z, y, core = row // NZ, lax.rem(row, NZ), col // 2, lax.rem(col, 2)

    basis_copy = pltpu.make_async_copy(basis_hbm, basis_ref, local_sem.at[0])
    basis_copy.start()
    inv_copy = pltpu.make_async_copy(inv_hbm, inv_ref, local_sem.at[1])
    inv_copy.start()

    around = [(lax.rem(row + N_ROW + a, N_ROW), lax.rem(col + N_COL + b, N_COL)) for a, b in AROUND]
    along_y = [(row, lax.rem(y + k, NY) * 2 + core) for k in range(1, NY)]
    along_z = [(x * NZ + lax.rem(z + k, NZ), col) for k in range(1, NZ)]
    along_x = [(lax.rem(x + k, NX) * NZ + z, col) for k in range(1, NX)]
    other = [(row, y * 2 + 1 - core)]
    partners = around + along_y + along_z + along_x + other
    barrier = pltpu.get_barrier_semaphore()
    for device in partners:
        pl.semaphore_signal(barrier, inc=1, device_id=device, device_id_type=MESH)

    lanes8 = lax.broadcasted_iota(I32, (8, 128), 1)
    rows8 = lax.broadcasted_iota(I32, (8, 128), 0)
    rows16 = lax.broadcasted_iota(I32, (16, 128), 0)
    nodes = rows16 * 128 + lax.broadcasted_iota(I32, (16, 128), 1)
    lane_row = lax.broadcasted_iota(I32, (1, 128), 1)
    pending = []

    low_col, high_col = col > 0, col < N_COL - 1
    low_row, high_row = row > 0, row < N_ROW - 1
    slots = []
    for source, which in ((side_sm, 0), (side_sm, 1), (end_sm, 0), (end_sm, 1)):
        place = jnp.full((16, 128), EMPTY, I32)
        for pos in range(SIDE):
            place = jnp.where(nodes == source[which, pos], pos, place)
        slots.append(place)
    corner_slot = jnp.full((16, 128), EMPTY, I32)
    list_ref[...] = jnp.zeros((8, 128), I32)
    list_ref[0:2, 0:SIDE] = side_ref[...] + 1
    list_ref[2:4, 0:SIDE] = end_ref[...] + 1
    listed = list_ref[...]
    for i in range(2):
        for j in range(2):
            both = (slots[i] != EMPTY) & (slots[2 + j] != EMPTY)
            number = jnp.max(jnp.max(jnp.where(both, nodes, -1), axis=0, keepdims=True), axis=1, keepdims=True)
            listed = jnp.where((rows8 == 4) & (lanes8 == 2 * i + j), number + 1, listed)
            corner_slot = jnp.where(both, 2 * (1 - i) + (1 - j), corner_slot)
    slots.append(corner_slot)
    for k in range(5):
        slot_ref[k] = slots[k]
    listed = listed + pltpu.roll(listed, GAP, 1) + pltpu.roll(listed, 2 * GAP, 1) - 1
    sample_of = (lanes8 >= GAP).astype(I32) + (lanes8 >= 2 * GAP).astype(I32)
    edge_key = jnp.where(listed >= 0, sample_of * 16 + (listed >> 7), -1)
    edge_low = jnp.where(listed >= 0, listed & 127, 0)

    def one(flag):
        return jnp.where(flag, 1.0, 0.0).astype(F32)

    def shared(place, there):
        return jnp.where(place != EMPTY, one(there), 0.0)

    copies = (1.0 + shared(slots[0], low_col) + shared(slots[1], high_col)) * (
        1.0 + shared(slots[2], low_row) + shared(slots[3], high_row)
    )
    weight = 1.0 / copies

    def edge_tile(vectors):
        tile = jnp.zeros((8, 128), F32)
        for s in range(SAMPLES):
            for h in range(NH):
                tile = jnp.where(edge_key == s * 16 + h, take(vectors[s][h : h + 1, :], edge_low), tile)
        return tile

    def halo_start(slot, vectors):
        halo_out[slot] = edge_tile(vectors)
        copies = []
        for k, device in enumerate(around):
            copy = pltpu.make_async_remote_copy(
                src_ref=halo_out.at[slot], dst_ref=halo_in.at[slot, k],
                send_sem=hs_sem.at[slot, k], recv_sem=hr_sem.at[slot, k],
                device_id=device, device_id_type=MESH,
            )
            copy.start()
            copies.append(copy)
        pending.extend(copies)
        return copies

    def halo_finish(slot, copies, vectors):
        for copy in copies:
            copy.wait_recv()
        arrived = []
        for k, which, there in ((7, 1, low_col), (6, 0, high_col), (5, 3, low_row), (4, 2, high_row)):
            arrived.append(jnp.where(there, halo_in[slot, k, which : which + 1, :], 0.0))
        corner = jnp.zeros((1, 128), F32)
        in_list = lane_row - jnp.where(lane_row >= 2 * GAP, 2 * GAP, jnp.where(lane_row >= GAP, GAP, 0))
        for i in range(2):
            for j in range(2):
                k = AROUND.index((1 - 2 * j, 1 - 2 * i))
                there = (high_col if i else low_col) & (high_row if j else low_row)
                found = jnp.where(there, halo_in[slot, k, 4:5, :], 0.0)
                corner = jnp.where(in_list == 2 * (1 - i) + (1 - j), found, corner)
        arrived.append(corner)
        result = []
        for s in range(SAMPLES):
            total = vectors[s]
            for k in range(5):
                total = total + take(arrived[k], slot_ref[k] + GAP * s)
            result.append(total)
        return result

    node_ref[...] = jnp.zeros((SAMPLES, 16, 128), F32)
    mass_vm[...] = jnp.ones((16, 128), F32)
    for h in range(NH):
        width = min(128, NL - 128 * h)
        mass_vm[h : h + 1, 0:width] = mass_ref[0:1, 128 * h : 128 * h + width]
        for s in range(SAMPLES):
            node_ref[s, h : h + 1, 0:width] = load_ref[s : s + 1, 128 * h : 128 * h + width]
    load = [node_ref[s] for s in range(SAMPLES)]
    mass = mass_vm[...]
    pl.semaphore_wait(barrier, len(partners))
    load_halo = halo_start(0, load)

    for p in range(3):
        for j in range(16):
            number = conn_ref[p : p + 1, 128 * j : 128 * j + 128]
            low = number & 127
            low_ref[p, j : j + 1, :] = low
            high_ref[p, j : j + 1, :] = number >> 7
            hot = jnp.where(lax.broadcasted_iota(I32, (128, 128), 0) == low, 1.0, 0.0)
            hot_ref[:, p * EL + 128 * j : p * EL + 128 * j + 128] = hot.astype(BF16)
    for k in range(4):
        for j in range(16):
            geo_ref[k, j : j + 1, :] = geom_ref[k : k + 1, 128 * j : 128 * j + 128]
    live = nodes < count_sm[0]
    for s in range(SAMPLES):
        grown = cover_ref[...] * jnp.exp(-rates_sm[s] * graze_ref[...])
        cond_ref[s] = jnp.where(live, grown, 0.0)

    def gradients():
        g0, g1, g2, g3 = (geo_ref[k] for k in range(4))
        return (g0, g1, -g0 - g1), (g2, g3, -g2 - g3)

    def scatter(terms):
        for s in range(SAMPLES):
            for p in range(3):
                high = terms[s][p].astype(BF16).astype(F32)
                piece_ref[s, 0, p] = high
                piece_ref[s, 1, p] = terms[s][p] - high
        for p in range(3):
            for j in range(16):
                here = high_ref[p, j : j + 1, :] == rows16
                for s in range(SAMPLES):
                    for q in range(2):
                        value = jnp.where(here, piece_ref[s, q, p, j : j + 1, :], 0.0)
                        left_ref[32 * s + 16 * q : 32 * s + 16 * q + 16, p * EL + 128 * j : p * EL + 128 * j + 128] = (
                            value.astype(BF16)
                        )
        summed = dot_lanes(left_ref[...], hot_ref[...])
        return [summed[32 * s : 32 * s + 16] + summed[32 * s + 16 : 32 * s + 32] for s in range(SAMPLES)]

    def operate(vectors):
        b_terms, c_terms = gradients()
        terms = []
        for s in range(SAMPLES):
            corner = []
            for p in range(3):
                low, high = low_ref[p], high_ref[p]
                value = jnp.zeros((16, 128), F32)
                for h in range(NH):
                    value = jnp.where(high == h, take(vectors[s][h : h + 1, :], low), value)
                corner.append(value)
            along_b = b_terms[0] * corner[0] + b_terms[1] * corner[1] + b_terms[2] * corner[2]
            along_c = c_terms[0] * corner[0] + c_terms[1] * corner[1] + c_terms[2] * corner[2]
            along_b, along_c = cond_ref[s] * along_b, cond_ref[s] * along_c
            terms.append([b_terms[p] * along_b + c_terms[p] * along_c for p in range(3)])
        summed = scatter(terms)
        return [mass * vectors[s] + summed[s] for s in range(SAMPLES)]

    b_terms, c_terms = gradients()
    squares = [b_terms[p] * b_terms[p] + c_terms[p] * c_terms[p] for p in range(3)]
    diag = scatter([[cond_ref[s] * squares[p] for p in range(3)] for s in range(SAMPLES)])
    diag = [mass + diag[s] for s in range(SAMPLES)]
    diag_halo = halo_start(1, diag)

    basis_copy.wait()
    wide_ref[...] = jnp.zeros((12 * NC, 128), F32)
    for h in range(NH):
        width = min(128, NL - 128 * h)
        wide_ref[NC * h : NC * h + NC, 0:width] = (
            basis_ref[:, 128 * h : 128 * h + width] * weight[h : h + 1, 0:width]
        )
    wide_high, wide_low = halves(wide_ref[...])
    spread_ref[0 : 12 * NC] = wide_high
    spread_ref[12 * NC : 24 * NC] = wide_low

    own_group = lax.broadcasted_iota(I32, (16, 12 * NC), 0) == lax.broadcasted_iota(I32, (16, 12 * NC), 1) // NC

    def restrict(vectors):
        stacked = jnp.concatenate(vectors, axis=0)
        high, low = halves(stacked)
        both = dot_lanes(jnp.concatenate([high, low], axis=0), spread_ref[...])
        both = both[0:48, 0 : 12 * NC] + both[48:96, 0 : 12 * NC] + both[0:48, 12 * NC : 24 * NC]
        result = []
        for s in range(SAMPLES):
            kept = jnp.where(own_group, both[16 * s : 16 * s + 16], 0.0)
            kept = jnp.sum(kept, axis=0, keepdims=True)
            result.append(over_groups(kept[:, 0:128] + kept[:, 128:256] + kept[:, 256:384]))
        return result

    def prolong(coarse):
        pieces = []
        for s in range(SAMPLES):
            line = coarse[s]
            line = jnp.concatenate([line, line, line], axis=1)
            pieces.append(jnp.where(own_group, jnp.broadcast_to(line, (16, 12 * NC)), 0.0))
        high, low = halves(jnp.concatenate(pieces, axis=0))
        first = dot_rows(jnp.concatenate([high, low], axis=0), spread_ref[0 : 12 * NC])
        total = first[0:48] + first[48:96] + dot_rows(high, spread_ref[12 * NC : 24 * NC])
        return [total[16 * s : 16 * s + 16] for s in range(SAMPLES)]

    def coarse_setup():
        inv_copy.wait()
        into = lax.broadcasted_iota(I32, (256, 256), 1)
        from_lane = ((into & 127) >> 5) * 64 + (into >> 7) * 32 + (into & 31)
        move = jnp.where(lax.broadcasted_iota(I32, (256, 256), 0) == from_lane, 1.0, 0.0).astype(BF16)
        for m in range(64):
            part, t = m % 8, m // 8
            moved = dot_rows(inv_ref[:, 256 * m : 256 * m + 256], move).astype(BF16)
            for c in range(2):
                coarse_ref[c, NC * part : NC * part + NC, 128 * t : 128 * t + 128] = moved[:, 128 * c : 128 * c + 128]

    part_mask = lax.broadcasted_iota(I32, (32, 256), 0) // 4 == lax.broadcasted_iota(I32, (32, 256), 1) // NC

    def coarse_half(turn, which):
        pieces = []
        for t in range(8):
            pieces.append(all_ref[turn, pl.ds(pl.multiple_of(which * 256 + 32 * t, 32), 32), :])
        high, low = halves(jnp.concatenate(pieces, axis=1))
        both = dot_lanes(jnp.concatenate([high, low], axis=0), coarse_ref[which])
        return both[0:32] + both[32:64]

    def everyone(turn, rhs, scalars, between=None):
        sample = rows8 & 3
        tile = jnp.where(sample == 0, rhs[0], jnp.where(sample == 1, rhs[1], jnp.where(sample == 2, rhs[2], scalars)))
        mine = (rows8 >> 2 == y // 4) & (lanes8 >> 5 == lax.rem(y, 4))
        first_ref[turn, y] = jnp.where(mine, tile, 0.0)

        def send(refs, sends, recvs, devices):
            copies = []
            for k, device in enumerate(devices):
                copy = pltpu.make_async_remote_copy(
                    src_ref=refs, dst_ref=refs, send_sem=sends.at[turn, k], recv_sem=recvs.at[turn, k],
                    device_id=device, device_id_type=MESH,
                )
                copy.start()
                copies.append(copy)
            pending.extend(copies)
            return copies

        def arrive(copies):
            for copy in copies:
                copy.wait_recv()

        copies = send(first_ref.at[turn, y], ys_sem, yr_sem, along_y)
        if between is not None:
            between()
        arrive(copies)
        block = first_ref[turn, 0]
        for k in range(1, NY):
            block = block + first_ref[turn, k]
        base = pl.multiple_of((core * 32 + x * 8 + z) * 8, 8)
        all_ref[turn, pl.ds(base, 8), :] = block
        arrive(send(all_ref.at[turn, pl.ds(base, 8)], zs_sem, zr_sem, along_z))
        base = pl.multiple_of((core * 32 + x * 8) * 8, 64)
        arrive(send(all_ref.at[turn, pl.ds(base, 64)], xs_sem, xr_sem, along_x))
        base = pl.multiple_of(core * 256, 256)
        copies = send(all_ref.at[turn, pl.ds(base, 256)], cs_sem, cr_sem, other)
        total = coarse_half(turn, core)
        arrive(copies)
        total = jnp.where(part_mask, total + coarse_half(turn, 1 - core), 0.0)
        total = jnp.sum(total.reshape(4, 8, 256), axis=0)
        total = over_groups(total[:, 0:128] + total[:, 128:256])
        coarse = [total[s : s + 1] + total[s + 4 : s + 5] for s in range(SAMPLES)]
        if turn == 0:
            return coarse, None
        sums = all_ref[turn, 0:8, :]
        for k in range(1, 64):
            sums = sums + all_ref[turn, 8 * k : 8 * k + 8, :]
        return coarse, over_groups(sums[3:4] + sums[7:8])

    def scalar_line(rows):
        stacked = jnp.zeros((16, 128), F32)
        for k, value in enumerate(rows):
            stacked = jnp.where(rows16 == k, value, stacked)
        summed = jnp.sum(stacked, axis=1, keepdims=True)
        placed = jnp.where(rows16 == (lax.broadcasted_iota(I32, (16, 128), 1) & 31), summed, 0.0)
        return jnp.sum(placed, axis=0, keepdims=True)

    def over_nodes(value):
        return jnp.sum(value, axis=0, keepdims=True)

    def fit_row(residual, scale, rhs, coarse, s):
        own = over_nodes(weight * residual * residual * scale)
        return own + jnp.where(lane_row < NC, rhs[s] * coarse[s], 0.0)

    samples = range(SAMPLES)

    residual = halo_finish(0, load_halo, load)
    rhs = restrict(residual)
    coarse, _ = everyone(0, rhs, jnp.zeros((1, 128), F32), coarse_setup)
    diag = halo_finish(1, diag_halo, diag)
    inverse_diag = [1.0 / diag[s] for s in samples]
    spread = prolong(coarse)
    copies = halo_start(2, spread)
    spread = halo_finish(2, copies, spread)
    precond = [residual[s] * inverse_diag[s] + spread[s] for s in samples]

    direction = precond
    raw = operate(direction)
    copies = halo_start(3, raw)
    line = scalar_line(
        [fit_row(residual[s], inverse_diag[s], rhs, coarse, s) for s in samples]
        + [over_nodes(direction[s] * raw[s]) for s in samples]
    )
    image = halo_finish(3, copies, raw)
    image_rhs = restrict(image)
    image_coarse, sums = everyone(1, image_rhs, line)
    fit = [sums[:, s : s + 1] for s in samples]
    curved = [sums[:, 3 + s : 4 + s] for s in samples]
    step = [fit[s] / curved[s] for s in samples]
    coarse = [coarse[s] - step[s] * image_coarse[s] for s in samples]
    spread = prolong(coarse)
    copies = halo_start(4, spread)
    solution = [step[s] * direction[s] for s in samples]
    residual = [residual[s] - step[s] * image[s] for s in samples]
    rhs = [rhs[s] - step[s] * image_rhs[s] for s in samples]
    spread = halo_finish(4, copies, spread)
    precond = [residual[s] * inverse_diag[s] + spread[s] for s in samples]

    fresh = operate(precond)
    copies = halo_start(5, fresh)
    line = scalar_line(
        [fit_row(residual[s], inverse_diag[s], rhs, coarse, s) for s in samples]
        + [over_nodes(precond[s] * fresh[s]) for s in samples]
        + [over_nodes(precond[s] * raw[s]) for s in samples]
    )
    fresh_image = halo_finish(5, copies, fresh)
    fresh_rhs = restrict(fresh_image)
    fresh_coarse, sums = everyone(2, fresh_rhs, line)
    fit_next = [sums[:, s : s + 1] for s in samples]
    ratio = [fit_next[s] / fit[s] for s in samples]
    curved = [
        sums[:, 3 + s : 4 + s] + ratio[s] * (2.0 * sums[:, 6 + s : 7 + s] + ratio[s] * curved[s]) for s in samples
    ]
    step = [fit_next[s] / curved[s] for s in samples]
    coarse = [coarse[s] - step[s] * (fresh_coarse[s] + ratio[s] * image_coarse[s]) for s in samples]
    spread = prolong(coarse)
    copies = halo_start(6, spread)
    solution = [solution[s] + step[s] * (precond[s] + ratio[s] * direction[s]) for s in samples]
    residual = [residual[s] - step[s] * (fresh_image[s] + ratio[s] * image[s]) for s in samples]

    def put(ref, values):
        for s in samples:
            for h in range(NH):
                width = min(128, NL - 128 * h)
                ref[s : s + 1, 128 * h : 128 * h + width] = values[s][h : h + 1, 0:width]

    put(sol_ref, solution)
    put(res_ref, residual)
    spread = halo_finish(6, copies, spread)
    put(pre_ref, [residual[s] * inverse_diag[s] + spread[s] for s in samples])
    for copy in pending:
        copy.wait_send()


def body(
    load, node_mass, side_lists, end_lists, connect, geometry, cover, grazing, rates, elem_count, basis, coarse_inverse
):
    vmem = pl.BlockSpec(memory_space=pltpu.VMEM)
    smem = pl.BlockSpec(memory_space=pltpu.SMEM)
    hbm = pl.BlockSpec(memory_space=pl.ANY)
    dma = pltpu.SemaphoreType.DMA
    return pl.pallas_call(
        kernel,
        out_shape=[jax.ShapeDtypeStruct((SAMPLES, NL), F32)] * 3,
        in_specs=[vmem, vmem, vmem, vmem, smem, smem, vmem, vmem, vmem, vmem, smem, smem, hbm, hbm],
        out_specs=[vmem] * 3,
        scratch_shapes=[
            pltpu.VMEM((NC, NL), F32),
            pltpu.VMEM((NC, 512 * NC), BF16),
            pltpu.VMEM((3, 16, 128), I32),
            pltpu.VMEM((3, 16, 128), I32),
            pltpu.VMEM((4, 16, 128), F32),
            pltpu.VMEM((SAMPLES, 16, 128), F32),
            pltpu.VMEM((SAMPLES, 2, 3, 16, 128), F32),
            pltpu.VMEM((96, 3 * EL), BF16),
            pltpu.VMEM((128, 3 * EL), BF16),
            pltpu.VMEM((16, 128), F32),
            pltpu.VMEM((5, 16, 128), I32),
            pltpu.VMEM((8, 128), I32),
            pltpu.VMEM((12 * NC, 128), F32),
            pltpu.VMEM((24 * NC, 128), BF16),
            pltpu.VMEM((2, 256, 1024), BF16),
            pltpu.VMEM((3, 512, 128), F32),
            pltpu.VMEM((3, NY, 8, 128), F32),
            pltpu.VMEM((SAMPLES, 16, 128), F32),
            pltpu.VMEM((HALOS, 8, 128), F32),
            pltpu.VMEM((HALOS, 8, 8, 128), F32),
            dma((2,)),
            dma((HALOS, 8)), dma((HALOS, 8)),
            dma((3, NY - 1)), dma((3, NY - 1)),
            dma((3, NZ - 1)), dma((3, NZ - 1)),
            dma((3, NX - 1)), dma((3, NX - 1)),
            dma((3, 1)), dma((3, 1)),
        ],
        compiler_params=pltpu.CompilerParams(
            collective_id=0, has_side_effects=True, vmem_limit_bytes=40 * 2**20
        ),
    )(
        load, node_mass.reshape(1, NL), side_lists, end_lists, side_lists, end_lists, connect, geometry,
        cover.reshape(16, 128), grazing.reshape(16, 128), rates, elem_count, basis, coarse_inverse,
    )


def solution(mesh):
    both = ("row", "col")
    return jax.shard_map(
        body,
        mesh=mesh,
        in_specs=(
            P(None, both), P(both), P(None, both), P(None, both), P(None, both), P(None, both),
            P(both), P(both), P(), P(both), P(None, both), P(both, None),
        ),
        out_specs=(P(None, both), P(None, both), P(None, both)),
        check_vma=False,
    )
```

time: 874 us -> 103 us (0.12)
  blocking collectives: 531 us -> 0 us
  other arithmetic: 169 us -> 0 us
  Pallas kernels: 0 us -> 92 us
  local copies, waits for them, and re-layouts: 87.5 us -> 9.58 us
  starting transfers between devices: 58.2 us -> 0 us
  waiting for transfers between devices: 17 us -> 0 us
    psum x3 -> x0, blocking collectives: 304 us -> none  [the longest x2 203 us: fit_sum(): lax.psum(jnp.sum(weight[None, :] * first * second, axis=1), ('row', 'col'))]
    all_gather x3 -> x0, blocking collectives: 227 us -> none  [precondition(): lax.all_gather(coarse_rhs, ('row', 'col'), axis=1, tiled=True)]
    scatter-add x27 -> x0, other arithmetic: 140 us -> none  [the longest x2 71 us: element_terms(): summed.at[:, connect.reshape(-1)]]
    pallas_call x0 -> x1, Pallas kernels: none -> 92 us  [body(): pl.pallas_call(kernel, out_shape=[jax.ShapeDtypeStruct((SAMPLES, NL), F32...]
    gather x46 -> x0, local copies, waits for them, and re-layouts: 68.2 us -> none  [the longest x2 41.8 us: element_terms(): corner = vector[:, connect]]
    ppermute x24 -> x0, starting transfers between devices: 58.2 us -> none  [the longest x12 35.4 us: with_halo(): lax.ppermute(tail, axis, [(i, (i + 1) % count) for i in range(ends)])]
    ppermute x24 -> x0, waiting for transfers between devices: 17 us -> none  [the longest x12 17 us: with_halo(): lax.ppermute(head, axis, [((i + 1) % count, i) for i in range(ends)])]
    mul x6 -> x0, other arithmetic: 13.2 us -> none  [the longest x2 9.15 us: element_terms(): conduct[:, None, :]]
  transfers between devices with their start and end apart: 24 -> 0, of which waited for: 11 -> 0; matrix products, arithmetic and copies ran while one was open for 2% -> 0% of each run, Pallas kernels for 0% -> 0%
where the time goes in v1:
time: 103 us
  Pallas kernels  92 us (89%)
  local copies, waits for them, and re-layouts  9.58 us (9%)
  between operations  1.31 us (1%)
    pallas_call x1, Pallas kernels, body(): pl.pallas_call(kernel, out_shape=[jax.ShapeDtypeStruct((SAMPLES, NL), F32...  92 us
    unnamed x23, local copies, waits for them, and re-layouts  8.88 us

profile of v1, /device:TPU:1, one launch (start us, length us, event | category | flops | bytes accessed | tf_op | source)
XLA Modules:
  0.0 102.9 jit_solution(6274466060966331252)
XLA Ops:
  0.6 0.0 copy-start.4
  1.3 0.7 reshape.15.mass_ref
  2.0 0.0 copy-done.4
  2.0 0.0 copy-start
  2.0 1.2 %copy-done = bf16[32,16384]{1,0:T(8,128)(2,1)S(1)} copy-done((bf16[32,16384]{1,0:T(8,128)(2,1)S(1)}, bf16[32,16384]{1,0:T(8,128)(2,1)}, u32[]{:S(2)}) %copy-start) | copy-done | bytes 1048600
  3.2 0.0 copy-start.1
  3.2 0.9 copy-done.1
  4.1 0.0 copy-start.2
  4.1 0.8 copy-done.2
  4.9 0.0 copy-start.3
  4.9 0.8 copy-done.3
  5.7 0.0 copy-start.5
  5.7 0.7 copy-done.5
  6.3 0.0 copy-start.6
  6.3 0.7 copy-done.6
  7.0 0.0 copy-start.7
  7.0 0.7 copy-done.7
  7.7 0.0 copy-start.8
  7.7 0.7 copy-done.8
  8.4 0.0 copy-start.9
  8.4 0.7 copy-done.9
  9.1 92.0 %shard_map.139 = (f32[3,1089]{1,0:T(4,128)S(1)}, f32[3,1089]{1,0:T(4,128)S(1)}, f32[3,1089]{1,0:T(4,128)S(1)}) custom-call(f32[3,1089]{1,0:T(4,128)S(1)} %copy-done.4, f32[1,1089]{1,0:T(1,128)S(1)} %reshape.15.mass_ref, s32[2,33]{1,0:T(2,128)S(1)} %copy-done.7, s32[2,33]{1,0:T(2,128)S(1)} %copy-done.8, s32[2,33]{1,0:T(2,128)S(1)} %copy-done.7, ...), custom_call_target="tpu_custom_call" | custom-call | tf_op jit(solution)/shard_map/pallas_call | solution.py:435
  101.1 0.6 copy.19
  101.7 0.6 copy.20
  102.3 0.6 copy.21
Async XLA Ops:
  0.6 1.4 %copy-start.4 = (f32[3,1089]{1,0:T(4,128)S(1)}, f32[3,1089]{1,0:T(4,128)}, u32[]{:S(2)}) copy-start(f32[3,1089]{1,0:T(4,128)} %load_ref.1) | copy-start | bytes 39208
  2.0 1.2 %copy-start = (bf16[32,16384]{1,0:T(8,128)(2,1)S(1)}, bf16[32,16384]{1,0:T(8,128)(2,1)}, u32[]{:S(2)}) copy-start(bf16[32,16384]{1,0:T(8,128)(2,1)} %inv_hbm.1) | copy-start | bytes 3145732
  3.2 0.9 copy-start.1
  4.1 0.8 copy-start.2
  4.9 0.8 copy-start.3
  5.7 0.7 copy-start.5
  6.3 0.7 copy-start.6
  7.0 0.7 copy-start.7
  7.7 0.7 copy-start.8
  8.4 0.7 copy-start.9

commit v2 on v1

--- a/solution.py
+++ b/solution.py
@@ -45,28 +45,36 @@
 
 
 def kernel(
+    load_hbm, mass_hbm, side_hbm, end_hbm, conn_hbm, geom_hbm, cover_hbm, graze_hbm,
+    rates_hbm, count_hbm, basis_hbm, inv_hbm,
+    sol_ref, res_ref, pre_ref,
     load_ref, mass_ref, side_ref, end_ref, side_sm, end_sm, conn_ref, geom_ref, cover_ref, graze_ref,
-    rates_sm, count_sm, basis_hbm, inv_hbm,
-    sol_ref, res_ref, pre_ref,
-    basis_ref, inv_ref, low_ref, high_ref, geo_ref, cond_ref, piece_ref, left_ref, hot_ref,
+    rates_sm, count_sm, basis_ref, inv_ref, low_ref, high_ref, geo_ref, cond_ref, piece_ref, left_ref, hot_ref,
     mass_vm, slot_ref, list_ref, wide_ref, spread_ref, coarse_ref, all_ref, first_ref, node_ref,
     halo_out, halo_in,
-    local_sem, hs_sem, hr_sem, ys_sem, yr_sem, zs_sem, zr_sem, xs_sem, xr_sem, cs_sem, cr_sem,
+    local_sem, hs_sem, hr_sem, ps_sem, pr_sem, zs_sem, zr_sem, cs_sem, cr_sem,
 ):
     row, col = lax.axis_index("row"), lax.axis_index("col")
     x, z, y, core = row // NZ, lax.rem(row, NZ), col // 2, lax.rem(col, 2)
 
-    basis_copy = pltpu.make_async_copy(basis_hbm, basis_ref, local_sem.at[0])
-    basis_copy.start()
-    inv_copy = pltpu.make_async_copy(inv_hbm, inv_ref, local_sem.at[1])
-    inv_copy.start()
+    loads = []
+    for source, target in (
+        (side_hbm, side_sm), (end_hbm, end_sm), (side_hbm, side_ref), (end_hbm, end_ref), (load_hbm, load_ref),
+        (mass_hbm, mass_ref), (conn_hbm, conn_ref), (geom_hbm, geom_ref), (cover_hbm, cover_ref),
+        (graze_hbm, graze_ref), (rates_hbm, rates_sm), (count_hbm, count_sm), (basis_hbm, basis_ref), (inv_hbm, inv_ref),
+    ):
+        loads.append(pltpu.make_async_copy(source, target, local_sem.at[len(loads)]))
+        loads[-1].start()
+    basis_copy, inv_copy = loads[12:]
 
     around = [(lax.rem(row + N_ROW + a, N_ROW), lax.rem(col + N_COL + b, N_COL)) for a, b in AROUND]
-    along_y = [(row, lax.rem(y + k, NY) * 2 + core) for k in range(1, NY)]
-    along_z = [(x * NZ + lax.rem(z + k, NZ), col) for k in range(1, NZ)]
-    along_x = [(lax.rem(x + k, NX) * NZ + z, col) for k in range(1, NX)]
+    offsets = sorted(
+        ((a, b) for a in range(NX) for b in range(NY) if a or b), key=lambda o: -min(o[0], NX - o[0]) - min(o[1], NY - o[1])
+    )
+    plane = [(lax.rem(x + a, NX) * NZ + z, lax.rem(y + b, NY) * 2 + core) for a, b in offsets]
+    along_z = [(x * NZ + lax.rem(z + k, NZ), col) for k in (4, 3, 5, 2, 6, 1, 7)]
     other = [(row, y * 2 + 1 - core)]
-    partners = around + along_y + along_z + along_x + other
+    partners = around + plane + along_z + other
     barrier = pltpu.get_barrier_semaphore()
     for device in partners:
         pl.semaphore_signal(barrier, inc=1, device_id=device, device_id_type=MESH)
@@ -78,6 +86,8 @@
     lane_row = lax.broadcasted_iota(I32, (1, 128), 1)
     pending = []
 
+    for copy in loads[:6]:
+        copy.wait()
     low_col, high_col = col > 0, col < N_COL - 1
     low_row, high_row = row > 0, row < N_ROW - 1
     slots = []
@@ -164,7 +174,7 @@
     mass_vm[...] = jnp.ones((16, 128), F32)
     for h in range(NH):
         width = min(128, NL - 128 * h)
-        mass_vm[h : h + 1, 0:width] = mass_ref[0:1, 128 * h : 128 * h + width]
+        mass_vm[h : h + 1, 0:width] = mass_ref[128 * h : 128 * h + width].reshape(1, width)
         for s in range(SAMPLES):
             node_ref[s, h : h + 1, 0:width] = load_ref[s : s + 1, 128 * h : 128 * h + width]
     load = [node_ref[s] for s in range(SAMPLES)]
@@ -172,6 +182,8 @@
     pl.semaphore_wait(barrier, len(partners))
     load_halo = halo_start(0, load)
 
+    for copy in loads[6:12]:
+        copy.wait()
     for p in range(3):
         for j in range(16):
             number = conn_ref[p : p + 1, 128 * j : 128 * j + 128]
@@ -276,7 +288,7 @@
         from_lane = ((into & 127) >> 5) * 64 + (into >> 7) * 32 + (into & 31)
         move = jnp.where(lax.broadcasted_iota(I32, (256, 256), 0) == from_lane, 1.0, 0.0).astype(BF16)
         for m in range(64):
-            part, t = m % 8, m // 8
+            part, t = m // 16 * 2 + m % 2, m // 2 % 8
             moved = dot_rows(inv_ref[:, 256 * m : 256 * m + 256], move).astype(BF16)
             for c in range(2):
                 coarse_ref[c, NC * part : NC * part + NC, 128 * t : 128 * t + 128] = moved[:, 128 * c : 128 * c + 128]
@@ -292,10 +304,10 @@
         return both[0:32] + both[32:64]
 
     def everyone(turn, rhs, scalars, between=None):
-        sample = rows8 & 3
-        tile = jnp.where(sample == 0, rhs[0], jnp.where(sample == 1, rhs[1], jnp.where(sample == 2, rhs[2], scalars)))
-        mine = (rows8 >> 2 == y // 4) & (lanes8 >> 5 == lax.rem(y, 4))
-        first_ref[turn, y] = jnp.where(mine, tile, 0.0)
+        rows4 = lax.broadcasted_iota(I32, (4, 128), 0)
+        tile = jnp.where(rows4 == 0, rhs[0], jnp.where(rows4 == 1, rhs[1], jnp.where(rows4 == 2, rhs[2], scalars)))
+        mine = lax.broadcasted_iota(I32, (4, 128), 1) >> 5 == lax.rem(y, 4)
+        first_ref[turn, x * NY + y] = jnp.where(mine, tile, 0.0)
 
         def send(refs, sends, recvs, devices):
             copies = []
@@ -313,18 +325,20 @@
             for copy in copies:
                 copy.wait_recv()
 
-        copies = send(first_ref.at[turn, y], ys_sem, yr_sem, along_y)
+        copies = send(first_ref.at[turn, x * NY + y], ps_sem, pr_sem, plane)
         if between is not None:
             between()
         arrive(copies)
-        block = first_ref[turn, 0]
-        for k in range(1, NY):
-            block = block + first_ref[turn, k]
-        base = pl.multiple_of((core * 32 + x * 8 + z) * 8, 8)
-        all_ref[turn, pl.ds(base, 8), :] = block
-        arrive(send(all_ref.at[turn, pl.ds(base, 8)], zs_sem, zr_sem, along_z))
-        base = pl.multiple_of((core * 32 + x * 8) * 8, 64)
-        arrive(send(all_ref.at[turn, pl.ds(base, 64)], xs_sem, xr_sem, along_x))
+        base = (core * NZ + z) * 32
+        for k in range(NX):
+            fours = []
+            for q in range(2):
+                four = first_ref[turn, k * NY + 4 * q]
+                for j in range(1, 4):
+                    four = four + first_ref[turn, k * NY + 4 * q + j]
+                fours.append(four)
+            all_ref[turn, pl.ds(pl.multiple_of(base + 8 * k, 8), 8), :] = jnp.concatenate(fours, axis=0)
+        arrive(send(all_ref.at[turn, pl.ds(pl.multiple_of(base, 32), 32)], zs_sem, zr_sem, along_z))
         base = pl.multiple_of(core * 256, 256)
         copies = send(all_ref.at[turn, pl.ds(base, 256)], cs_sem, cr_sem, other)
         total = coarse_half(turn, core)
@@ -429,15 +443,24 @@
     load, node_mass, side_lists, end_lists, connect, geometry, cover, grazing, rates, elem_count, basis, coarse_inverse
 ):
     vmem = pl.BlockSpec(memory_space=pltpu.VMEM)
-    smem = pl.BlockSpec(memory_space=pltpu.SMEM)
-    hbm = pl.BlockSpec(memory_space=pl.ANY)
+    hbm = pl.BlockSpec(memory_space=pltpu.HBM)
     dma = pltpu.SemaphoreType.DMA
     return pl.pallas_call(
         kernel,
         out_shape=[jax.ShapeDtypeStruct((SAMPLES, NL), F32)] * 3,
-        in_specs=[vmem, vmem, vmem, vmem, smem, smem, vmem, vmem, vmem, vmem, smem, smem, hbm, hbm],
+        in_specs=[hbm] * 12,
         out_specs=[vmem] * 3,
         scratch_shapes=[
+            pltpu.VMEM((SAMPLES, NL), F32),
+            pltpu.VMEM((NL,), F32),
+            pltpu.VMEM((2, SIDE), I32), pltpu.VMEM((2, SIDE), I32),
+            pltpu.SMEM((2, SIDE), I32), pltpu.SMEM((2, SIDE), I32),
+            pltpu.VMEM((3, EL), I32),
+            pltpu.VMEM((4, EL), F32),
+            pltpu.VMEM((16, 128), F32),
+            pltpu.VMEM((16, 128), F32),
+            pltpu.SMEM((SAMPLES,), F32),
+            pltpu.SMEM((1,), I32),
             pltpu.VMEM((NC, NL), F32),
             pltpu.VMEM((NC, 512 * NC), BF16),
             pltpu.VMEM((3, 16, 128), I32),
@@ -454,22 +477,21 @@
             pltpu.VMEM((24 * NC, 128), BF16),
             pltpu.VMEM((2, 256, 1024), BF16),
             pltpu.VMEM((3, 512, 128), F32),
-            pltpu.VMEM((3, NY, 8, 128), F32),
+            pltpu.VMEM((3, NX * NY, 4, 128), F32),
             pltpu.VMEM((SAMPLES, 16, 128), F32),
             pltpu.VMEM((HALOS, 8, 128), F32),
             pltpu.VMEM((HALOS, 8, 8, 128), F32),
-            dma((2,)),
+            dma((14,)),
             dma((HALOS, 8)), dma((HALOS, 8)),
-            dma((3, NY - 1)), dma((3, NY - 1)),
+            dma((3, NX * NY - 1)), dma((3, NX * NY - 1)),
             dma((3, NZ - 1)), dma((3, NZ - 1)),
-            dma((3, NX - 1)), dma((3, NX - 1)),
             dma((3, 1)), dma((3, 1)),
         ],
         compiler_params=pltpu.CompilerParams(
-            collective_id=0, has_side_effects=True, vmem_limit_bytes=40 * 2**20
+            collective_id=0, has_side_effects=True, vmem_limit_bytes=56 * 2**20
         ),
     )(
-        load, node_mass.reshape(1, NL), side_lists, end_lists, side_lists, end_lists, connect, geometry,
+        load, node_mass, side_lists, end_lists, connect, geometry,
         cover.reshape(16, 128), grazing.reshape(16, 128), rates, elem_count, basis, coarse_inverse,
     )
 

time: 103 us -> 91.4 us (0.89)
  local copies, waits for them, and re-layouts: 9.58 us -> 2.68 us
  Pallas kernels: 92 us -> 87.2 us
    unnamed x23 -> x7, local copies, waits for them, and re-layouts: 8.88 us -> 2.68 us
    pallas_call x1, Pallas kernels: 92 us -> 87.2 us  [body(): pl.pallas_call(kernel, out_shape=[jax.ShapeDtypeStruct((SAMPLES, NL), F32...]
where the time goes in v2:
time: 91.4 us; the launch traced here: 91.2 us
  Pallas kernels  87.2 us (95%)
  local copies, waits for them, and re-layouts  2.68 us (3%)
  between operations  1.3 us (1%)
    pallas_call x1, Pallas kernels, body(): pl.pallas_call(kernel, out_shape=[jax.ShapeDtypeStruct((SAMPLES, NL), F32...  87.2 us
    unnamed x7, local copies, waits for them, and re-layouts  2.68 us

profile of v2, /device:TPU:1, one launch (start us, length us, event | category | flops | bytes accessed | tf_op | source)
XLA Modules:
  0.0 91.2 jit_solution(14003753314822163959)
XLA Ops:
  1.3 87.2 %shard_map.139 = (f32[3,1089]{1,0:T(4,128)}, f32[3,1089]{1,0:T(4,128)}, f32[3,1089]{1,0:T(4,128)}) custom-call(f32[3,1089]{1,0:T(4,128)} %load_hbm.1, f32[1089]{0:T(1024)} %mass_hbm.1, s32[2,33]{1,0:T(2,128)} %side_hbm.1, s32[2,33]{1,0:T(2,128)} %end_hbm.1, s32[3,2048]{1,0:T(4,128)} %conn_hbm.1, f32[4,2048]{1,0:T(4,128)} %geom_hbm.1, f32[16,128]{1,0:T(8,128)} %bitcast.2, ...), custom_call_target="tpu_custom_call" | custom-call | tf_op jit(solution)/shard_map/pallas_call | solution.py:448
  88.5 0.0 copy-start.1
  88.5 1.3 %copy.19 = f32[3,1089]{1,0:T(4,128)} copy(f32[3,1089]{1,0:T(4,128)} %get-tuple-element.6) | data formatting | bytes 26136
  89.8 0.0 copy-done.1
  89.8 0.0 copy-start
  89.8 0.6 copy.20
  90.5 0.1 copy-done
  90.6 0.6 copy.21
Async XLA Ops:
  88.5 1.3 %copy-start.1 = (f32[3,1089]{1,0:T(4,128)S(1)}, f32[3,1089]{1,0:T(4,128)}, u32[]{:S(2)}) copy-start(f32[3,1089]{1,0:T(4,128)} %get-tuple-element.7) | copy-start | bytes 39208
  89.8 0.7 copy-start

commit v3 on v2

--- a/solution.py
+++ b/solution.py
@@ -17,7 +17,8 @@
 GAP = 40
 EMPTY = 36
 AROUND = ((-1, -1), (-1, 1), (1, -1), (1, 1), (-1, 0), (1, 0), (0, -1), (0, 1))
-HALOS = 7
+HALOS = 4
+BLOCKS = 3 * 4 * NC
 
 
 def take(row, index):
@@ -47,12 +48,12 @@
 def kernel(
     load_hbm, mass_hbm, side_hbm, end_hbm, conn_hbm, geom_hbm, cover_hbm, graze_hbm,
     rates_hbm, count_hbm, basis_hbm, inv_hbm,
-    sol_ref, res_ref, pre_ref,
+    out_ref,
     load_ref, mass_ref, side_ref, end_ref, side_sm, end_sm, conn_ref, geom_ref, cover_ref, graze_ref,
     rates_sm, count_sm, basis_ref, inv_ref, low_ref, high_ref, geo_ref, cond_ref, piece_ref, left_ref, hot_ref,
     mass_vm, slot_ref, list_ref, wide_ref, spread_ref, coarse_ref, all_ref, first_ref, node_ref,
-    halo_out, halo_in,
-    local_sem, hs_sem, hr_sem, ps_sem, pr_sem, zs_sem, zr_sem, cs_sem, cr_sem,
+    halo_out, halo_in, rim_ref, rims_ref, near_ref, swap_out, swap_in, part_out, part_in,
+    local_sem, hs_sem, hr_sem, ps_sem, pr_sem, zs_sem, zr_sem, cs_sem, cr_sem, es_sem, er_sem, ts_sem, tr_sem,
 ):
     row, col = lax.axis_index("row"), lax.axis_index("col")
     x, z, y, core = row // NZ, lax.rem(row, NZ), col // 2, lax.rem(col, 2)
@@ -73,8 +74,23 @@
     )
     plane = [(lax.rem(x + a, NX) * NZ + z, lax.rem(y + b, NY) * 2 + core) for a, b in offsets]
     along_z = [(x * NZ + lax.rem(z + k, NZ), col) for k in (4, 3, 5, 2, 6, 1, 7)]
-    other = [(row, y * 2 + 1 - core)]
-    partners = around + plane + along_z + other
+    other = (row, y * 2 + 1 - core)
+    readers = []
+    for a in (-1, 1, 0):
+        at_row = lax.rem(row + N_ROW + a, N_ROW)
+        place = (1 - a) * 4 + core
+        readers.append(((at_row, lax.rem(y + NY - 1, NY) * 2 + 1), place + 2))
+        readers.append(((at_row, lax.rem(y + 1, NY) * 2), place))
+        if a:
+            readers.append(((at_row, y * 2), place + 2))
+            readers.append(((at_row, y * 2 + 1), place))
+        else:
+            readers.append((other, place + 2 * core))
+    own_place = 4 + (1 - core) * 2 + core
+    beyond = [
+        (lax.rem(row + N_ROW + a, N_ROW), lax.rem(col + N_COL + b, N_COL)) for a in (-1, 0, 1) for b in (-2, 2)
+    ]
+    partners = around + plane + along_z + [other] + beyond
     barrier = pltpu.get_barrier_semaphore()
     for device in partners:
         pl.semaphore_signal(barrier, inc=1, device_id=device, device_id_type=MESH)
@@ -110,6 +126,13 @@
     slots.append(corner_slot)
     for k in range(5):
         slot_ref[k] = slots[k]
+    slot_ref[5] = jnp.where(slots[1] != EMPTY, slots[1] + GAP, slots[0])
+    slot_ref[6] = jnp.where(slots[3] != EMPTY, slots[3] + GAP, slots[2])
+    slot_ref[7] = jnp.where(corner_slot != EMPTY, corner_slot + 2 * GAP, EMPTY)
+    rim_lists = (
+        listed[1:2] + pltpu.roll(listed[0:1], GAP, 1) + pltpu.roll(listed[4:5], 2 * GAP, 1) - 1,
+        listed[3:4] + pltpu.roll(listed[2:3], GAP, 1) - 1,
+    )
     listed = listed + pltpu.roll(listed, GAP, 1) + pltpu.roll(listed, 2 * GAP, 1) - 1
     sample_of = (lanes8 >= GAP).astype(I32) + (lanes8 >= 2 * GAP).astype(I32)
     edge_key = jnp.where(listed >= 0, sample_of * 16 + (listed >> 7), -1)
@@ -282,31 +305,86 @@
         total = first[0:48] + first[48:96] + dot_rows(high, spread_ref[12 * NC : 24 * NC])
         return [total[16 * s : 16 * s + 16] for s in range(SAMPLES)]
 
-    def coarse_setup():
+    def rims_start():
+        for t in range(2):
+            index = jnp.broadcast_to(rim_lists[t], (NC, 128))
+            low = jnp.where(index >= 0, index & 127, 0)
+            high = jnp.where(index >= 0, index >> 7, -1)
+            value = jnp.zeros((NC, 128), F32)
+            for h in range(NH):
+                value = jnp.where(high == h, take(wide_ref[NC * h : NC * h + NC, :], low), value)
+            rim_ref[t] = value
+        copies = []
+        for k, (a, b) in enumerate(AROUND):
+            copy = pltpu.make_async_remote_copy(
+                src_ref=rim_ref.at[1 if b == 0 else 0], dst_ref=rims_ref.at[k], send_sem=es_sem.at[k],
+                recv_sem=er_sem.at[k], device_id=around[k], device_id_type=MESH,
+            )
+            copy.start()
+            copies.append(copy)
+        pending.extend(copies)
+        setups.extend(copies)
+
+    def swap_start():
         inv_copy.wait()
         into = lax.broadcasted_iota(I32, (256, 256), 1)
         from_lane = ((into & 127) >> 5) * 64 + (into >> 7) * 32 + (into & 31)
         move = jnp.where(lax.broadcasted_iota(I32, (256, 256), 0) == from_lane, 1.0, 0.0).astype(BF16)
+        first_core = core == 0
         for m in range(64):
             part, t = m // 16 * 2 + m % 2, m // 2 % 8
-            moved = dot_rows(inv_ref[:, 256 * m : 256 * m + 256], move).astype(BF16)
-            for c in range(2):
-                coarse_ref[c, NC * part : NC * part + NC, 128 * t : 128 * t + 128] = moved[:, 128 * c : 128 * c + 128]
-
-    part_mask = lax.broadcasted_iota(I32, (32, 256), 0) // 4 == lax.broadcasted_iota(I32, (32, 256), 1) // NC
-
-    def coarse_half(turn, which):
-        pieces = []
-        for t in range(8):
-            pieces.append(all_ref[turn, pl.ds(pl.multiple_of(which * 256 + 32 * t, 32), 32), :])
-        high, low = halves(jnp.concatenate(pieces, axis=1))
-        both = dot_lanes(jnp.concatenate([high, low], axis=0), coarse_ref[which])
-        return both[0:32] + both[32:64]
-
-    def everyone(turn, rhs, scalars, between=None):
-        rows4 = lax.broadcasted_iota(I32, (4, 128), 0)
-        tile = jnp.where(rows4 == 0, rhs[0], jnp.where(rows4 == 1, rhs[1], jnp.where(rows4 == 2, rhs[2], scalars)))
-        mine = lax.broadcasted_iota(I32, (4, 128), 1) >> 5 == lax.rem(y, 4)
+            moved = dot_rows(inv_ref[:, 256 * m : 256 * m + 256], move)
+            zero, one_ = moved[:, 0:128], moved[:, 128:256]
+            rows, lanes = slice(NC * part, NC * part + NC), slice(128 * t, 128 * t + 128)
+            coarse_ref[rows, lanes] = jnp.where(first_core, zero, one_).astype(BF16)
+            swap_out[rows, lanes] = jnp.where(first_core, one_, zero)
+        copy = pltpu.make_async_remote_copy(
+            src_ref=swap_out, dst_ref=swap_in, send_sem=cs_sem.at[0], recv_sem=cr_sem.at[0],
+            device_id=other, device_id_type=MESH,
+        )
+        copy.start()
+        pending.append(copy)
+        setups.append(copy)
+
+    def setup_start():
+        rims_start()
+        swap_start()
+
+    def setup_finish():
+        for copy in setups:
+            copy.wait_recv()
+        coarse_ref[256:512, :] = swap_in[...].astype(BF16)
+        lanes32 = lax.broadcasted_iota(I32, (NC, 128), 1)
+        for k in range(2):
+            near_ref[k] = jnp.zeros((BLOCKS, 256), BF16)
+        for k, (a, b) in enumerate(AROUND):
+            if a == 0 or b == 0:
+                start = 0 if a + b == 1 else GAP
+                kept = (lanes32 >= start) & (lanes32 < start + SIDE)
+            else:
+                i, j = (1 - b) // 2, (1 - a) // 2
+                kept = lanes32 == 2 * GAP + 2 * (1 - i) + (1 - j)
+            if a:
+                kept = kept & (low_row if a == 1 else high_row)
+            if b:
+                kept = kept & (low_col if b == 1 else high_col)
+            high, low = halves(jnp.where(kept, rims_ref[k], 0.0))
+            at = 128 * (1 - a) + NC * (1 - b)
+            lane = 128 if b == 0 else 0
+            near_ref[0, at : at + NC, lane : lane + 128] = high
+            near_ref[1, at : at + NC, lane : lane + 128] = low
+
+    setups = []
+    part_mask = lax.broadcasted_iota(I32, (32, 512), 0) // 4 == (lax.broadcasted_iota(I32, (32, 512), 1) & 255) // NC
+    lanes4 = lax.broadcasted_iota(I32, (4, 128), 1)
+    rows4 = lax.broadcasted_iota(I32, (4, 128), 0)
+
+    def by_sample(values):
+        return jnp.where(rows4 == 0, values[0], jnp.where(rows4 == 1, values[1], values[2]))
+
+    def everyone(turn, rhs, scalars, between=None, later=None):
+        tile = jnp.where(rows4 == 3, scalars, by_sample(rhs))
+        mine = lanes4 >> 5 == lax.rem(y, 4)
         first_ref[turn, x * NY + y] = jnp.where(mine, tile, 0.0)
 
         def send(refs, sends, recvs, devices):
@@ -338,21 +416,68 @@
                     four = four + first_ref[turn, k * NY + 4 * q + j]
                 fours.append(four)
             all_ref[turn, pl.ds(pl.multiple_of(base + 8 * k, 8), 8), :] = jnp.concatenate(fours, axis=0)
-        arrive(send(all_ref.at[turn, pl.ds(pl.multiple_of(base, 32), 32)], zs_sem, zr_sem, along_z))
-        base = pl.multiple_of(core * 256, 256)
-        copies = send(all_ref.at[turn, pl.ds(base, 256)], cs_sem, cr_sem, other)
-        total = coarse_half(turn, core)
+        copies = send(all_ref.at[turn, pl.ds(pl.multiple_of(base, 32), 32)], zs_sem, zr_sem, along_z)
+        if later is not None:
+            later()
         arrive(copies)
-        total = jnp.where(part_mask, total + coarse_half(turn, 1 - core), 0.0)
-        total = jnp.sum(total.reshape(4, 8, 256), axis=0)
-        total = over_groups(total[:, 0:128] + total[:, 128:256])
-        coarse = [total[s : s + 1] + total[s + 4 : s + 5] for s in range(SAMPLES)]
-        if turn == 0:
-            return coarse, None
-        sums = all_ref[turn, 0:8, :]
-        for k in range(1, 64):
-            sums = sums + all_ref[turn, 8 * k : 8 * k + 8, :]
-        return coarse, over_groups(sums[3:4] + sums[7:8])
+        half = pl.multiple_of(core * 256, 256)
+        gathered = [all_ref[turn, pl.ds(pl.multiple_of(half + 32 * t, 32), 32), :] for t in range(8)]
+        high, low = halves(jnp.concatenate(gathered, axis=1))
+        total = dot_lanes(jnp.concatenate([high, low], axis=0), coarse_ref[...])
+        total = jnp.where(part_mask, total[0:32] + total[32:64], 0.0)
+        total = total[0:8] + total[8:16] + total[16:24] + total[24:32]
+        total = total[0:4] + total[4:8]
+        mine = over_groups(total[:, 0:128] + total[:, 128:256])
+        others = over_groups(total[:, 256:384] + total[:, 384:512])
+        tile = jnp.where(lanes4 >> 5 == core, mine, jnp.where(lanes4 >> 5 == 1 - core, others, 0.0))
+        if turn:
+            sums = gathered[0]
+            for piece in gathered[1:]:
+                sums = sums + piece
+            sums = sums[0:8] + sums[8:16] + sums[16:24] + sums[24:32]
+            sums = over_groups(sums[3:4] + sums[7:8])
+            tile = jnp.where(rows4 == 3, jnp.where(lanes4 < 32, sums, 0.0), tile)
+        else:
+            tile = jnp.where(rows4 == 3, 0.0, tile)
+        part_out[turn] = tile
+        part_in[turn, own_place] = tile
+        for k, (device, place) in enumerate(readers):
+            copy = pltpu.make_async_remote_copy(
+                src_ref=part_out.at[turn], dst_ref=part_in.at[turn, place], send_sem=ts_sem.at[turn, k],
+                recv_sem=tr_sem.at[turn, place], device_id=device, device_id_type=MESH,
+            )
+            copy.start()
+            pending.append(copy)
+
+    def everyone_finish(turn):
+        for place in (0, 1, 2, 3, 8, 9, 10, 11, 4, 7, 5 + core):
+            pltpu.make_async_remote_copy(
+                src_ref=part_out.at[turn], dst_ref=part_in.at[turn, place], send_sem=ts_sem.at[turn, 0],
+                recv_sem=tr_sem.at[turn, place], device_id=other, device_id_type=MESH,
+            ).wait_recv()
+        tiles = []
+        for k in range(3):
+            left = part_in[turn, 4 * k] + part_in[turn, 4 * k + 1]
+            right = part_in[turn, 4 * k + 2] + part_in[turn, 4 * k + 3]
+            if k == 1:
+                sums = jnp.where(core == 0, right, left)[3:4]
+            whole = left + pltpu.roll(right, 64, 1)
+            tiles.append(jnp.where(core == 0, pltpu.roll(whole, 96, 1), whole))
+        return tiles, sums
+
+    def own_coarse(tiles):
+        own = over_groups(jnp.where(lanes4 >> 5 == 1, tiles[1], 0.0))
+        return [own[s : s + 1] for s in range(SAMPLES)]
+
+    def spread_all(tiles):
+        values = prolong(own_coarse(tiles))
+        high, low = halves(jnp.concatenate(tiles, axis=1))
+        both = dot_rows(jnp.concatenate([high, low], axis=0), near_ref[0])
+        both = both[0:4] + both[4:8] + dot_rows(high, near_ref[1])
+        for s in range(SAMPLES):
+            side, end = both[s : s + 1, 0:128], both[s : s + 1, 128:256]
+            values[s] = values[s] + take(side, slot_ref[5]) + take(side, slot_ref[7]) + take(end, slot_ref[6])
+        return values
 
     def scalar_line(rows):
         stacked = jnp.zeros((16, 128), F32)
@@ -373,68 +498,69 @@
 
     residual = halo_finish(0, load_halo, load)
     rhs = restrict(residual)
-    coarse, _ = everyone(0, rhs, jnp.zeros((1, 128), F32), coarse_setup)
+    everyone(0, rhs, jnp.zeros((1, 128), F32), setup_start, setup_finish)
     diag = halo_finish(1, diag_halo, diag)
     inverse_diag = [1.0 / diag[s] for s in samples]
-    spread = prolong(coarse)
-    copies = halo_start(2, spread)
-    spread = halo_finish(2, copies, spread)
+    tiles, _ = everyone_finish(0)
+    spread = spread_all(tiles)
     precond = [residual[s] * inverse_diag[s] + spread[s] for s in samples]
 
     direction = precond
     raw = operate(direction)
-    copies = halo_start(3, raw)
+    copies = halo_start(2, raw)
+    coarse = own_coarse(tiles)
     line = scalar_line(
         [fit_row(residual[s], inverse_diag[s], rhs, coarse, s) for s in samples]
         + [over_nodes(direction[s] * raw[s]) for s in samples]
     )
-    image = halo_finish(3, copies, raw)
+    image = halo_finish(2, copies, raw)
     image_rhs = restrict(image)
-    image_coarse, sums = everyone(1, image_rhs, line)
+    everyone(1, image_rhs, line)
+    image_tiles, sums = everyone_finish(1)
     fit = [sums[:, s : s + 1] for s in samples]
     curved = [sums[:, 3 + s : 4 + s] for s in samples]
     step = [fit[s] / curved[s] for s in samples]
-    coarse = [coarse[s] - step[s] * image_coarse[s] for s in samples]
-    spread = prolong(coarse)
-    copies = halo_start(4, spread)
+    steps = by_sample(step)
+    tiles = [tiles[k] - steps * image_tiles[k] for k in range(3)]
+    spread = spread_all(tiles)
     solution = [step[s] * direction[s] for s in samples]
     residual = [residual[s] - step[s] * image[s] for s in samples]
     rhs = [rhs[s] - step[s] * image_rhs[s] for s in samples]
-    spread = halo_finish(4, copies, spread)
     precond = [residual[s] * inverse_diag[s] + spread[s] for s in samples]
 
     fresh = operate(precond)
-    copies = halo_start(5, fresh)
+    copies = halo_start(3, fresh)
+    coarse = own_coarse(tiles)
     line = scalar_line(
         [fit_row(residual[s], inverse_diag[s], rhs, coarse, s) for s in samples]
         + [over_nodes(precond[s] * fresh[s]) for s in samples]
         + [over_nodes(precond[s] * raw[s]) for s in samples]
     )
-    fresh_image = halo_finish(5, copies, fresh)
+    fresh_image = halo_finish(3, copies, fresh)
     fresh_rhs = restrict(fresh_image)
-    fresh_coarse, sums = everyone(2, fresh_rhs, line)
+    everyone(2, fresh_rhs, line)
+    fresh_tiles, sums = everyone_finish(2)
     fit_next = [sums[:, s : s + 1] for s in samples]
     ratio = [fit_next[s] / fit[s] for s in samples]
     curved = [
         sums[:, 3 + s : 4 + s] + ratio[s] * (2.0 * sums[:, 6 + s : 7 + s] + ratio[s] * curved[s]) for s in samples
     ]
     step = [fit_next[s] / curved[s] for s in samples]
-    coarse = [coarse[s] - step[s] * (fresh_coarse[s] + ratio[s] * image_coarse[s]) for s in samples]
-    spread = prolong(coarse)
-    copies = halo_start(6, spread)
+    steps, ratios = by_sample(step), by_sample(ratio)
+    tiles = [tiles[k] - steps * (fresh_tiles[k] + ratios * image_tiles[k]) for k in range(3)]
+    spread = spread_all(tiles)
     solution = [solution[s] + step[s] * (precond[s] + ratio[s] * direction[s]) for s in samples]
     residual = [residual[s] - step[s] * (fresh_image[s] + ratio[s] * image[s]) for s in samples]
 
-    def put(ref, values):
+    def put(at, values):
         for s in samples:
             for h in range(NH):
                 width = min(128, NL - 128 * h)
-                ref[s : s + 1, 128 * h : 128 * h + width] = values[s][h : h + 1, 0:width]
-
-    put(sol_ref, solution)
-    put(res_ref, residual)
-    spread = halo_finish(6, copies, spread)
-    put(pre_ref, [residual[s] * inverse_diag[s] + spread[s] for s in samples])
+                out_ref[3 * at + s : 3 * at + s + 1, 128 * h : 128 * h + width] = values[s][h : h + 1, 0:width]
+
+    put(0, solution)
+    put(1, residual)
+    put(2, [residual[s] * inverse_diag[s] + spread[s] for s in samples])
     for copy in pending:
         copy.wait_send()
 
@@ -445,11 +571,11 @@
     vmem = pl.BlockSpec(memory_space=pltpu.VMEM)
     hbm = pl.BlockSpec(memory_space=pltpu.HBM)
     dma = pltpu.SemaphoreType.DMA
-    return pl.pallas_call(
+    whole = pl.pallas_call(
         kernel,
-        out_shape=[jax.ShapeDtypeStruct((SAMPLES, NL), F32)] * 3,
+        out_shape=[jax.ShapeDtypeStruct((3 * SAMPLES, NL), F32)],
         in_specs=[hbm] * 12,
-        out_specs=[vmem] * 3,
+        out_specs=[vmem],
         scratch_shapes=[
             pltpu.VMEM((SAMPLES, NL), F32),
             pltpu.VMEM((NL,), F32),
@@ -471,21 +597,28 @@
             pltpu.VMEM((96, 3 * EL), BF16),
             pltpu.VMEM((128, 3 * EL), BF16),
             pltpu.VMEM((16, 128), F32),
-            pltpu.VMEM((5, 16, 128), I32),
+            pltpu.VMEM((8, 16, 128), I32),
             pltpu.VMEM((8, 128), I32),
             pltpu.VMEM((12 * NC, 128), F32),
             pltpu.VMEM((24 * NC, 128), BF16),
-            pltpu.VMEM((2, 256, 1024), BF16),
+            pltpu.VMEM((512, 1024), BF16),
             pltpu.VMEM((3, 512, 128), F32),
             pltpu.VMEM((3, NX * NY, 4, 128), F32),
             pltpu.VMEM((SAMPLES, 16, 128), F32),
             pltpu.VMEM((HALOS, 8, 128), F32),
             pltpu.VMEM((HALOS, 8, 8, 128), F32),
+            pltpu.VMEM((2, NC, 128), F32),
+            pltpu.VMEM((8, NC, 128), F32),
+            pltpu.VMEM((2, BLOCKS, 256), BF16),
+            pltpu.VMEM((256, 1024), F32), pltpu.VMEM((256, 1024), F32),
+            pltpu.VMEM((3, 4, 128), F32), pltpu.VMEM((3, 12, 4, 128), F32),
             dma((14,)),
             dma((HALOS, 8)), dma((HALOS, 8)),
             dma((3, NX * NY - 1)), dma((3, NX * NY - 1)),
             dma((3, NZ - 1)), dma((3, NZ - 1)),
-            dma((3, 1)), dma((3, 1)),
+            dma((1,)), dma((1,)),
+            dma((8,)), dma((8,)),
+            dma((3, 11)), dma((3, 12)),
         ],
         compiler_params=pltpu.CompilerParams(
             collective_id=0, has_side_effects=True, vmem_limit_bytes=56 * 2**20
@@ -493,7 +626,8 @@
     )(
         load, node_mass, side_lists, end_lists, connect, geometry,
         cover.reshape(16, 128), grazing.reshape(16, 128), rates, elem_count, basis, coarse_inverse,
-    )
+    )[0]
+    return whole[0:3], whole[3:6], whole[6:9]
 
 
 def solution(mesh):

time: 91.4 us -> 90 us (0.985)
  local copies, waits for them, and re-layouts: 2.68 us -> 1.59 us
    unnamed x7 -> x0, local copies, waits for them, and re-layouts: 2.68 us -> none
    slice x0 -> x1, local copies, waits for them, and re-layouts: none -> 1.59 us  [body(): return (whole[0:3], whole[3:6], whole[6:9])]
where the time goes in v3:
time: 90 us; the launch traced here: 89.8 us
  Pallas kernels  86.9 us (97%)
  local copies, waits for them, and re-layouts  1.59 us (2%)
  between operations  1.29 us (1%)
    pallas_call x1, Pallas kernels, body(): pl.pallas_call(kernel, out_shape=[jax.ShapeDtypeStruct((3 * SAMPLES, NL),...  86.9 us

profile of v3, /device:TPU:1, one launch (start us, length us, event | category | flops | bytes accessed | tf_op | source)
XLA Modules:
  0.0 89.8 jit_solution(1394675783614159497)
XLA Ops:
  1.3 86.9 %shard_map.139 = f32[9,1089]{1,0:T(8,128)} custom-call(f32[3,1089]{1,0:T(4,128)} %load_hbm.1, f32[1089]{0:T(1024)} %mass_hbm.1, s32[2,33]{1,0:T(2,128)} %side_hbm.1, s32[2,33]{1,0:T(2,128)} %end_hbm.1, s32[3,2048]{1,0:T(4,128)} %conn_hbm.1, f32[4,2048]{1,0:T(4,128)} %geom_hbm.1, f32[16,128]{1,0:T(8,128)} %bitcast.2, f32[16,128]{1,0:T(8,128)} %bitcast.3, ...), custom_call_target="tpu_custom_call" | custom-call | tf_op jit(solution)/shard_map/pallas_call | solution.py:574
  88.2 1.6 %fusion = (f32[3,1089]{1,0:T(4,128)}, f32[3,1089]{1,0:T(4,128)}, f32[3,1089]{1,0:T(4,128)}) fusion(f32[9,1089]{1,0:T(8,128)} %shard_map.139), kind=kLoop, calls=%fused_computation | loop fusion | bytes 78408 | tf_op jit(solution)/shard_map/slice | solution.py:630

commit v4 on v3

--- a/solution.py
+++ b/solution.py
@@ -38,6 +38,13 @@
 
 def dot_rows(left, right):
     return lax.dot_general(left, right, (((1,), (0,)), ((), ())), preferred_element_type=F32)
+
+
+def wait_all(whole, sem, device, sent=False):
+    copy = pltpu.make_async_remote_copy(
+        src_ref=whole, dst_ref=whole, send_sem=sem, recv_sem=sem, device_id=device, device_id_type=MESH
+    )
+    (copy.wait_send if sent else copy.wait_recv)()
 
 
 def over_groups(row):
@@ -76,12 +83,13 @@
     along_z = [(x * NZ + lax.rem(z + k, NZ), col) for k in (4, 3, 5, 2, 6, 1, 7)]
     other = (row, y * 2 + 1 - core)
     readers = []
-    for a in (-1, 1, 0):
+    for a, b in ((-1, 1), (1, 1), (-1, 0), (1, 0), (0, 1), (0, 0)):
         at_row = lax.rem(row + N_ROW + a, N_ROW)
         place = (1 - a) * 4 + core
-        readers.append(((at_row, lax.rem(y + NY - 1, NY) * 2 + 1), place + 2))
-        readers.append(((at_row, lax.rem(y + 1, NY) * 2), place))
-        if a:
+        if b:
+            readers.append(((at_row, lax.rem(y + NY - 1, NY) * 2 + 1), place + 2))
+            readers.append(((at_row, lax.rem(y + 1, NY) * 2), place))
+        elif a:
             readers.append(((at_row, y * 2), place + 2))
             readers.append(((at_row, y * 2 + 1), place))
         else:
@@ -158,21 +166,16 @@
 
     def halo_start(slot, vectors):
         halo_out[slot] = edge_tile(vectors)
-        copies = []
         for k, device in enumerate(around):
-            copy = pltpu.make_async_remote_copy(
+            pltpu.make_async_remote_copy(
                 src_ref=halo_out.at[slot], dst_ref=halo_in.at[slot, k],
-                send_sem=hs_sem.at[slot, k], recv_sem=hr_sem.at[slot, k],
+                send_sem=hs_sem.at[slot], recv_sem=hr_sem.at[slot],
                 device_id=device, device_id_type=MESH,
-            )
-            copy.start()
-            copies.append(copy)
-        pending.extend(copies)
-        return copies
-
-    def halo_finish(slot, copies, vectors):
-        for copy in copies:
-            copy.wait_recv()
+            ).start()
+        pending.append((halo_in.at[slot], hs_sem.at[slot]))
+
+    def halo_finish(slot, vectors):
+        wait_all(halo_in.at[slot], hr_sem.at[slot], other)
         arrived = []
         for k, which, there in ((7, 1, low_col), (6, 0, high_col), (5, 3, low_row), (4, 2, high_row)):
             arrived.append(jnp.where(there, halo_in[slot, k, which : which + 1, :], 0.0))
@@ -203,7 +206,7 @@
     load = [node_ref[s] for s in range(SAMPLES)]
     mass = mass_vm[...]
     pl.semaphore_wait(barrier, len(partners))
-    load_halo = halo_start(0, load)
+    halo_start(0, load)
 
     for copy in loads[6:12]:
         copy.wait()
@@ -267,7 +270,7 @@
     squares = [b_terms[p] * b_terms[p] + c_terms[p] * c_terms[p] for p in range(3)]
     diag = scatter([[cond_ref[s] * squares[p] for p in range(3)] for s in range(SAMPLES)])
     diag = [mass + diag[s] for s in range(SAMPLES)]
-    diag_halo = halo_start(1, diag)
+    halo_start(1, diag)
 
     basis_copy.wait()
     wide_ref[...] = jnp.zeros((12 * NC, 128), F32)
@@ -314,16 +317,12 @@
             for h in range(NH):
                 value = jnp.where(high == h, take(wide_ref[NC * h : NC * h + NC, :], low), value)
             rim_ref[t] = value
-        copies = []
         for k, (a, b) in enumerate(AROUND):
-            copy = pltpu.make_async_remote_copy(
-                src_ref=rim_ref.at[1 if b == 0 else 0], dst_ref=rims_ref.at[k], send_sem=es_sem.at[k],
-                recv_sem=er_sem.at[k], device_id=around[k], device_id_type=MESH,
-            )
-            copy.start()
-            copies.append(copy)
-        pending.extend(copies)
-        setups.extend(copies)
+            pltpu.make_async_remote_copy(
+                src_ref=rim_ref.at[1 if b == 0 else 0], dst_ref=rims_ref.at[k], send_sem=es_sem.at[0],
+                recv_sem=er_sem.at[0], device_id=around[k], device_id_type=MESH,
+            ).start()
+        pending.append((rims_ref, es_sem.at[0]))
 
     def swap_start():
         inv_copy.wait()
@@ -338,21 +337,19 @@
             rows, lanes = slice(NC * part, NC * part + NC), slice(128 * t, 128 * t + 128)
             coarse_ref[rows, lanes] = jnp.where(first_core, zero, one_).astype(BF16)
             swap_out[rows, lanes] = jnp.where(first_core, one_, zero)
-        copy = pltpu.make_async_remote_copy(
+        pltpu.make_async_remote_copy(
             src_ref=swap_out, dst_ref=swap_in, send_sem=cs_sem.at[0], recv_sem=cr_sem.at[0],
             device_id=other, device_id_type=MESH,
-        )
-        copy.start()
-        pending.append(copy)
-        setups.append(copy)
+        ).start()
+        pending.append((swap_out, cs_sem.at[0]))
 
     def setup_start():
         rims_start()
         swap_start()
 
     def setup_finish():
-        for copy in setups:
-            copy.wait_recv()
+        wait_all(rims_ref, er_sem.at[0], other)
+        wait_all(swap_in, cr_sem.at[0], other)
         coarse_ref[256:512, :] = swap_in[...].astype(BF16)
         lanes32 = lax.broadcasted_iota(I32, (NC, 128), 1)
         for k in range(2):
@@ -374,7 +371,6 @@
             near_ref[0, at : at + NC, lane : lane + 128] = high
             near_ref[1, at : at + NC, lane : lane + 128] = low
 
-    setups = []
     part_mask = lax.broadcasted_iota(I32, (32, 512), 0) // 4 == (lax.broadcasted_iota(I32, (32, 512), 1) & 255) // NC
     lanes4 = lax.broadcasted_iota(I32, (4, 128), 1)
     rows4 = lax.broadcasted_iota(I32, (4, 128), 0)
@@ -387,26 +383,19 @@
         mine = lanes4 >> 5 == lax.rem(y, 4)
         first_ref[turn, x * NY + y] = jnp.where(mine, tile, 0.0)
 
-        def send(refs, sends, recvs, devices):
-            copies = []
-            for k, device in enumerate(devices):
-                copy = pltpu.make_async_remote_copy(
-                    src_ref=refs, dst_ref=refs, send_sem=sends.at[turn, k], recv_sem=recvs.at[turn, k],
+        def send(refs, whole, sends, recvs, devices):
+            for device in devices:
+                pltpu.make_async_remote_copy(
+                    src_ref=refs, dst_ref=refs, send_sem=sends.at[turn], recv_sem=recvs.at[turn],
                     device_id=device, device_id_type=MESH,
-                )
-                copy.start()
-                copies.append(copy)
-            pending.extend(copies)
-            return copies
-
-        def arrive(copies):
-            for copy in copies:
-                copy.wait_recv()
-
-        copies = send(first_ref.at[turn, x * NY + y], ps_sem, pr_sem, plane)
+                ).start()
+            pending.append((whole, sends.at[turn]))
+
+        whole = first_ref.at[turn, pl.ds(0, NX * NY - 1)]
+        send(first_ref.at[turn, x * NY + y], whole, ps_sem, pr_sem, plane)
         if between is not None:
             between()
-        arrive(copies)
+        wait_all(whole, pr_sem.at[turn], other)
         base = (core * NZ + z) * 32
         for k in range(NX):
             fours = []
@@ -416,10 +405,11 @@
                     four = four + first_ref[turn, k * NY + 4 * q + j]
                 fours.append(four)
             all_ref[turn, pl.ds(pl.multiple_of(base + 8 * k, 8), 8), :] = jnp.concatenate(fours, axis=0)
-        copies = send(all_ref.at[turn, pl.ds(pl.multiple_of(base, 32), 32)], zs_sem, zr_sem, along_z)
+        whole = all_ref.at[turn, pl.ds(0, 32 * (NZ - 1))]
+        send(all_ref.at[turn, pl.ds(pl.multiple_of(base, 32), 32)], whole, zs_sem, zr_sem, along_z)
         if later is not None:
             later()
-        arrive(copies)
+        wait_all(whole, zr_sem.at[turn], other)
         half = pl.multiple_of(core * 256, 256)
         gathered = [all_ref[turn, pl.ds(pl.multiple_of(half + 32 * t, 32), 32), :] for t in range(8)]
         high, low = halves(jnp.concatenate(gathered, axis=1))
@@ -441,20 +431,15 @@
             tile = jnp.where(rows4 == 3, 0.0, tile)
         part_out[turn] = tile
         part_in[turn, own_place] = tile
-        for k, (device, place) in enumerate(readers):
-            copy = pltpu.make_async_remote_copy(
-                src_ref=part_out.at[turn], dst_ref=part_in.at[turn, place], send_sem=ts_sem.at[turn, k],
-                recv_sem=tr_sem.at[turn, place], device_id=device, device_id_type=MESH,
-            )
-            copy.start()
-            pending.append(copy)
+        for device, place in readers:
+            pltpu.make_async_remote_copy(
+                src_ref=part_out.at[turn], dst_ref=part_in.at[turn, place], send_sem=ts_sem.at[turn],
+                recv_sem=tr_sem.at[turn], device_id=device, device_id_type=MESH,
+            ).start()
+        pending.append((part_in.at[turn, pl.ds(0, 11)], ts_sem.at[turn]))
 
     def everyone_finish(turn):
-        for place in (0, 1, 2, 3, 8, 9, 10, 11, 4, 7, 5 + core):
-            pltpu.make_async_remote_copy(
-                src_ref=part_out.at[turn], dst_ref=part_in.at[turn, place], send_sem=ts_sem.at[turn, 0],
-                recv_sem=tr_sem.at[turn, place], device_id=other, device_id_type=MESH,
-            ).wait_recv()
+        wait_all(part_in.at[turn, pl.ds(0, 11)], tr_sem.at[turn], other)
         tiles = []
         for k in range(3):
             left = part_in[turn, 4 * k] + part_in[turn, 4 * k + 1]
@@ -496,10 +481,10 @@
 
     samples = range(SAMPLES)
 
-    residual = halo_finish(0, load_halo, load)
+    residual = halo_finish(0, load)
     rhs = restrict(residual)
     everyone(0, rhs, jnp.zeros((1, 128), F32), setup_start, setup_finish)
-    diag = halo_finish(1, diag_halo, diag)
+    diag = halo_finish(1, diag)
     inverse_diag = [1.0 / diag[s] for s in samples]
     tiles, _ = everyone_finish(0)
     spread = spread_all(tiles)
@@ -507,13 +492,13 @@
 
     direction = precond
     raw = operate(direction)
-    copies = halo_start(2, raw)
+    halo_start(2, raw)
     coarse = own_coarse(tiles)
     line = scalar_line(
         [fit_row(residual[s], inverse_diag[s], rhs, coarse, s) for s in samples]
         + [over_nodes(direction[s] * raw[s]) for s in samples]
     )
-    image = halo_finish(2, copies, raw)
+    image = halo_finish(2, raw)
     image_rhs = restrict(image)
     everyone(1, image_rhs, line)
     image_tiles, sums = everyone_finish(1)
@@ -529,14 +514,14 @@
     precond = [residual[s] * inverse_diag[s] + spread[s] for s in samples]
 
     fresh = operate(precond)
-    copies = halo_start(3, fresh)
+    halo_start(3, fresh)
     coarse = own_coarse(tiles)
     line = scalar_line(
         [fit_row(residual[s], inverse_diag[s], rhs, coarse, s) for s in samples]
         + [over_nodes(precond[s] * fresh[s]) for s in samples]
         + [over_nodes(precond[s] * raw[s]) for s in samples]
     )
-    fresh_image = halo_finish(3, copies, fresh)
+    fresh_image = halo_finish(3, fresh)
     fresh_rhs = restrict(fresh_image)
     everyone(2, fresh_rhs, line)
     fresh_tiles, sums = everyone_finish(2)
@@ -556,13 +541,13 @@
         for s in samples:
             for h in range(NH):
                 width = min(128, NL - 128 * h)
-                out_ref[3 * at + s : 3 * at + s + 1, 128 * h : 128 * h + width] = values[s][h : h + 1, 0:width]
+                out_ref[at, s : s + 1, 128 * h : 128 * h + width] = values[s][h : h + 1, 0:width]
 
     put(0, solution)
     put(1, residual)
     put(2, [residual[s] * inverse_diag[s] + spread[s] for s in samples])
-    for copy in pending:
-        copy.wait_send()
+    for whole, sem in pending:
+        wait_all(whole, sem, other, sent=True)
 
 
 def body(
@@ -573,7 +558,7 @@
     dma = pltpu.SemaphoreType.DMA
     whole = pl.pallas_call(
         kernel,
-        out_shape=[jax.ShapeDtypeStruct((3 * SAMPLES, NL), F32)],
+        out_shape=[jax.ShapeDtypeStruct((3, SAMPLES, NL), F32)],
         in_specs=[hbm] * 12,
         out_specs=[vmem],
         scratch_shapes=[
@@ -613,12 +598,12 @@
             pltpu.VMEM((256, 1024), F32), pltpu.VMEM((256, 1024), F32),
             pltpu.VMEM((3, 4, 128), F32), pltpu.VMEM((3, 12, 4, 128), F32),
             dma((14,)),
-            dma((HALOS, 8)), dma((HALOS, 8)),
-            dma((3, NX * NY - 1)), dma((3, NX * NY - 1)),
-            dma((3, NZ - 1)), dma((3, NZ - 1)),
+            dma((HALOS,)), dma((HALOS,)),
+            dma((3,)), dma((3,)),
+            dma((3,)), dma((3,)),
             dma((1,)), dma((1,)),
-            dma((8,)), dma((8,)),
-            dma((3, 11)), dma((3, 12)),
+            dma((1,)), dma((1,)),
+            dma((3,)), dma((3,)),
         ],
         compiler_params=pltpu.CompilerParams(
             collective_id=0, has_side_effects=True, vmem_limit_bytes=56 * 2**20
@@ -627,7 +612,7 @@
         load, node_mass, side_lists, end_lists, connect, geometry,
         cover.reshape(16, 128), grazing.reshape(16, 128), rates, elem_count, basis, coarse_inverse,
     )[0]
-    return whole[0:3], whole[3:6], whole[6:9]
+    return whole[0], whole[1], whole[2]
 
 
 def solution(mesh):

time: 90 us -> 86.1 us (0.957)
  Pallas kernels: 86.9 us -> 83.3 us
    pallas_call x1, Pallas kernels: 86.9 us -> 83.3 us  [body(): pl.pallas_call(kernel, out_shape=[jax.ShapeDtypeStruct((3, SAMPLES, NL),...]
    slice x1 -> x0, local copies, waits for them, and re-layouts: 1.59 us -> none  [body(): return (whole[0:3], whole[3:6], whole[6:9])]
    squeeze x0 -> x1, local copies, waits for them, and re-layouts: none -> 1.38 us  [body(): return (whole[0], whole[1], whole[2])]
where the time goes in v4:
time: 86.1 us; the launch traced here: 85.9 us
  Pallas kernels  83.3 us (97%)
  local copies, waits for them, and re-layouts  1.38 us (2%)
  between operations  1.29 us (1%)
    pallas_call x1, Pallas kernels, body(): pl.pallas_call(kernel, out_shape=[jax.ShapeDtypeStruct((3, SAMPLES, NL),...  83.3 us

profile of v4, /device:TPU:1, one launch (start us, length us, event | category | flops | bytes accessed | tf_op | source)
XLA Modules:
  0.0 85.9 jit_solution(14305070005912304651)
XLA Ops:
  1.3 83.3 %shard_map.139 = f32[3,3,1089]{2,1,0:T(4,128)} custom-call(f32[3,1089]{1,0:T(4,128)} %load_hbm.1, f32[1089]{0:T(1024)} %mass_hbm.1, s32[2,33]{1,0:T(2,128)} %side_hbm.1, s32[2,33]{1,0:T(2,128)} %end_hbm.1, s32[3,2048]{1,0:T(4,128)} %conn_hbm.1, f32[4,2048]{1,0:T(4,128)} %geom_hbm.1, f32[16,128]{1,0:T(8,128)} %bitcast.8, f32[16,128]{1,0:T(8,128)} %bitcast.9, ...), custom_call_target="tpu_custom_call" | custom-call | tf_op jit(solution)/shard_map/pallas_call | solution.py:559
  84.6 1.4 %slice_bitcast_fusion = (f32[3,1089]{1,0:T(4,128)}, f32[3,1089]{1,0:T(4,128)}, f32[3,1089]{1,0:T(4,128)}) fusion(f32[3,3,1089]{2,1,0:T(4,128)} %shard_map.139), kind=kLoop, calls=%fused_computation | loop fusion | bytes 78408 | tf_op jit(solution)/shard_map/squeeze | solution.py:615

commit v5 on v4

--- a/solution.py
+++ b/solution.py
@@ -60,7 +60,7 @@
     rates_sm, count_sm, basis_ref, inv_ref, low_ref, high_ref, geo_ref, cond_ref, piece_ref, left_ref, hot_ref,
     mass_vm, slot_ref, list_ref, wide_ref, spread_ref, coarse_ref, all_ref, first_ref, node_ref,
     halo_out, halo_in, rim_ref, rims_ref, near_ref, swap_out, swap_in, part_out, part_in,
-    local_sem, hs_sem, hr_sem, ps_sem, pr_sem, zs_sem, zr_sem, cs_sem, cr_sem, es_sem, er_sem, ts_sem, tr_sem,
+    local_sem, hs_sem, hr_sem, ps_sem, pr_sem, zs_sem, zr_sem, fs_sem, fr_sem, cs_sem, cr_sem, es_sem, er_sem, ts_sem, tr_sem,
 ):
     row, col = lax.axis_index("row"), lax.axis_index("col")
     x, z, y, core = row // NZ, lax.rem(row, NZ), col // 2, lax.rem(col, 2)
@@ -72,7 +72,8 @@
         (graze_hbm, graze_ref), (rates_hbm, rates_sm), (count_hbm, count_sm), (basis_hbm, basis_ref), (inv_hbm, inv_ref),
     ):
         loads.append(pltpu.make_async_copy(source, target, local_sem.at[len(loads)]))
-        loads[-1].start()
+    for copy in loads[:6]:
+        copy.start()
     basis_copy, inv_copy = loads[12:]
 
     around = [(lax.rem(row + N_ROW + a, N_ROW), lax.rem(col + N_COL + b, N_COL)) for a, b in AROUND]
@@ -95,13 +96,14 @@
         else:
             readers.append((other, place + 2 * core))
     own_place = 4 + (1 - core) * 2 + core
-    beyond = [
-        (lax.rem(row + N_ROW + a, N_ROW), lax.rem(col + N_COL + b, N_COL)) for a in (-1, 0, 1) for b in (-2, 2)
-    ]
-    partners = around + plane + along_z + [other] + beyond
+    beyond = [(lax.rem(row + N_ROW + a, N_ROW), lax.rem(col + N_COL + b, N_COL)) for a in (-1, 1) for b in (-2, 2)]
+    partners = around + beyond + plane + along_z
     barrier = pltpu.get_barrier_semaphore()
     for device in partners:
         pl.semaphore_signal(barrier, inc=1, device_id=device, device_id_type=MESH)
+
+    for copy in loads[6:]:
+        copy.start()
 
     lanes8 = lax.broadcasted_iota(I32, (8, 128), 1)
     rows8 = lax.broadcasted_iota(I32, (8, 128), 0)
@@ -216,8 +218,10 @@
             low = number & 127
             low_ref[p, j : j + 1, :] = low
             high_ref[p, j : j + 1, :] = number >> 7
-            hot = jnp.where(lax.broadcasted_iota(I32, (128, 128), 0) == low, 1.0, 0.0)
-            hot_ref[:, p * EL + 128 * j : p * EL + 128 * j + 128] = hot.astype(BF16)
+        lows = low_ref[p].astype(F32).T
+        for j in range(16):
+            hot = jnp.where(lax.broadcasted_iota(I32, (128, 128), 1).astype(F32) == lows[:, j : j + 1], 1.0, 0.0)
+            hot_ref[p * EL + 128 * j : p * EL + 128 * j + 128, :] = hot.astype(BF16)
     for k in range(4):
         for j in range(16):
             geo_ref[k, j : j + 1, :] = geom_ref[k : k + 1, 128 * j : 128 * j + 128]
@@ -245,7 +249,7 @@
                         left_ref[32 * s + 16 * q : 32 * s + 16 * q + 16, p * EL + 128 * j : p * EL + 128 * j + 128] = (
                             value.astype(BF16)
                         )
-        summed = dot_lanes(left_ref[...], hot_ref[...])
+        summed = dot_rows(left_ref[...], hot_ref[...])
         return [summed[32 * s : 32 * s + 16] + summed[32 * s + 16 : 32 * s + 32] for s in range(SAMPLES)]
 
     def operate(vectors):
@@ -334,9 +338,9 @@
             part, t = m // 16 * 2 + m % 2, m // 2 % 8
             moved = dot_rows(inv_ref[:, 256 * m : 256 * m + 256], move)
             zero, one_ = moved[:, 0:128], moved[:, 128:256]
-            rows, lanes = slice(NC * part, NC * part + NC), slice(128 * t, 128 * t + 128)
-            coarse_ref[rows, lanes] = jnp.where(first_core, zero, one_).astype(BF16)
-            swap_out[rows, lanes] = jnp.where(first_core, one_, zero)
+            rows = slice(NC * part, NC * part + NC)
+            coarse_ref[t, rows, :] = jnp.where(first_core, zero, one_).astype(BF16)
+            swap_out[t, rows, :] = jnp.where(first_core, one_, zero)
         pltpu.make_async_remote_copy(
             src_ref=swap_out, dst_ref=swap_in, send_sem=cs_sem.at[0], recv_sem=cr_sem.at[0],
             device_id=other, device_id_type=MESH,
@@ -350,7 +354,7 @@
     def setup_finish():
         wait_all(rims_ref, er_sem.at[0], other)
         wait_all(swap_in, cr_sem.at[0], other)
-        coarse_ref[256:512, :] = swap_in[...].astype(BF16)
+        coarse_ref[:, 256:512, :] = swap_in[...].astype(BF16)
         lanes32 = lax.broadcasted_iota(I32, (NC, 128), 1)
         for k in range(2):
             near_ref[k] = jnp.zeros((BLOCKS, 256), BF16)
@@ -405,15 +409,26 @@
                     four = four + first_ref[turn, k * NY + 4 * q + j]
                 fours.append(four)
             all_ref[turn, pl.ds(pl.multiple_of(base + 8 * k, 8), 8), :] = jnp.concatenate(fours, axis=0)
-        whole = all_ref.at[turn, pl.ds(0, 32 * (NZ - 1))]
-        send(all_ref.at[turn, pl.ds(pl.multiple_of(base, 32), 32)], whole, zs_sem, zr_sem, along_z)
+        block = all_ref.at[turn, pl.ds(pl.multiple_of(base, 32), 32)]
+        far, near = all_ref.at[turn, pl.ds(0, 96)], all_ref.at[turn, pl.ds(0, 128)]
+        send(block, far, fs_sem, fr_sem, along_z[:3])
+        send(block, near, zs_sem, zr_sem, along_z[3:])
         if later is not None:
             later()
-        wait_all(whole, zr_sem.at[turn], other)
-        half = pl.multiple_of(core * 256, 256)
-        gathered = [all_ref[turn, pl.ds(pl.multiple_of(half + 32 * t, 32), 32), :] for t in range(8)]
-        high, low = halves(jnp.concatenate(gathered, axis=1))
-        total = dot_lanes(jnp.concatenate([high, low], axis=0), coarse_ref[...])
+        half = core * 256
+        wait_all(near, zr_sem.at[turn], other)
+        total, sums = None, None
+        for steps in ((0, 2, 6, 1, 7), (4, 3, 5)):
+            at = [lax.rem(z + k, NZ) for k in steps]
+            if total is not None:
+                wait_all(far, fr_sem.at[turn], other)
+            gathered = [all_ref[turn, pl.ds(pl.multiple_of(half + 32 * t, 32), 32), :] for t in at]
+            high, low = halves(jnp.concatenate(gathered, axis=1))
+            inverse = jnp.concatenate([coarse_ref[t] for t in at], axis=1)
+            product = dot_lanes(jnp.concatenate([high, low], axis=0), inverse)
+            total = product if total is None else total + product
+            for piece in gathered:
+                sums = piece if sums is None else sums + piece
         total = jnp.where(part_mask, total[0:32] + total[32:64], 0.0)
         total = total[0:8] + total[8:16] + total[16:24] + total[24:32]
         total = total[0:4] + total[4:8]
@@ -421,9 +436,6 @@
         others = over_groups(total[:, 256:384] + total[:, 384:512])
         tile = jnp.where(lanes4 >> 5 == core, mine, jnp.where(lanes4 >> 5 == 1 - core, others, 0.0))
         if turn:
-            sums = gathered[0]
-            for piece in gathered[1:]:
-                sums = sums + piece
             sums = sums[0:8] + sums[8:16] + sums[16:24] + sums[24:32]
             sums = over_groups(sums[3:4] + sums[7:8])
             tile = jnp.where(rows4 == 3, jnp.where(lanes4 < 32, sums, 0.0), tile)
@@ -580,13 +592,13 @@
             pltpu.VMEM((SAMPLES, 16, 128), F32),
             pltpu.VMEM((SAMPLES, 2, 3, 16, 128), F32),
             pltpu.VMEM((96, 3 * EL), BF16),
-            pltpu.VMEM((128, 3 * EL), BF16),
+            pltpu.VMEM((3 * EL, 128), BF16),
             pltpu.VMEM((16, 128), F32),
             pltpu.VMEM((8, 16, 128), I32),
             pltpu.VMEM((8, 128), I32),
             pltpu.VMEM((12 * NC, 128), F32),
             pltpu.VMEM((24 * NC, 128), BF16),
-            pltpu.VMEM((512, 1024), BF16),
+            pltpu.VMEM((NZ, 512, 128), BF16),
             pltpu.VMEM((3, 512, 128), F32),
             pltpu.VMEM((3, NX * NY, 4, 128), F32),
             pltpu.VMEM((SAMPLES, 16, 128), F32),
@@ -595,10 +607,11 @@
             pltpu.VMEM((2, NC, 128), F32),
             pltpu.VMEM((8, NC, 128), F32),
             pltpu.VMEM((2, BLOCKS, 256), BF16),
-            pltpu.VMEM((256, 1024), F32), pltpu.VMEM((256, 1024), F32),
+            pltpu.VMEM((NZ, 256, 128), F32), pltpu.VMEM((NZ, 256, 128), F32),
             pltpu.VMEM((3, 4, 128), F32), pltpu.VMEM((3, 12, 4, 128), F32),
             dma((14,)),
             dma((HALOS,)), dma((HALOS,)),
+            dma((3,)), dma((3,)),
             dma((3,)), dma((3,)),
             dma((3,)), dma((3,)),
             dma((1,)), dma((1,)),

time: 86.1 us -> 86 us (level)
  no operation moved by 1% of the time
where the time goes in v5:
time: 86 us; the launch traced here: 85.7 us
  Pallas kernels  83.1 us (97%)
  local copies, waits for them, and re-layouts  1.38 us (2%)
  between operations  1.29 us (2%)
    pallas_call x1, Pallas kernels, body(): pl.pallas_call(kernel, out_shape=[jax.ShapeDtypeStruct((3, SAMPLES, NL),...  83.1 us

profile of v5, /device:TPU:1, one launch (start us, length us, event | category | flops | bytes accessed | tf_op | source)
XLA Modules:
  0.0 85.7 jit_solution(6880520739164880433)
XLA Ops:
  1.3 83.1 %shard_map.139 = f32[3,3,1089]{2,1,0:T(4,128)} custom-call(f32[3,1089]{1,0:T(4,128)} %load_hbm.1, f32[1089]{0:T(1024)} %mass_hbm.1, s32[2,33]{1,0:T(2,128)} %side_hbm.1, s32[2,33]{1,0:T(2,128)} %end_hbm.1, s32[3,2048]{1,0:T(4,128)} %conn_hbm.1, f32[4,2048]{1,0:T(4,128)} %geom_hbm.1, f32[16,128]{1,0:T(8,128)} %bitcast.8, f32[16,128]{1,0:T(8,128)} %bitcast.9, ...), custom_call_target="tpu_custom_call" | custom-call | tf_op jit(solution)/shard_map/pallas_call | solution.py:571
  84.3 1.4 %slice_bitcast_fusion = (f32[3,1089]{1,0:T(4,128)}, f32[3,1089]{1,0:T(4,128)}, f32[3,1089]{1,0:T(4,128)}) fusion(f32[3,3,1089]{2,1,0:T(4,128)} %shard_map.139), kind=kLoop, calls=%fused_computation | loop fusion | bytes 78408 | tf_op jit(solution)/shard_map/squeeze | solution.py:628
